TPU v7x, 256 devices: a whole 4x4x8 slice. The times are simulated.
256 devices in a mesh: tensor: 16 (over y_lo, z), draw: 4 (over x), batch: 4 (over y_hi, core).
Axes of the slice: x: 4, y: 4 (y_hi: 2, y_lo: 2; y = y_hi * 2 + y_lo), z: 8, core: 2. Of those that a mesh axis runs over, the one named last changes fastest.
Arguments:
- tokens: bfloat16 [4, 512, 4608], P('draw', None, ('batch', 'tensor')), may hold values from -6 to 6
- cotangent: bfloat16 [4, 512, 4608], P('draw', None, ('batch', 'tensor')), may hold values from -6 to 6
- gate_up_weight: bfloat16 [2, 4608, 18432], P(None, 'batch', ('tensor', 'draw')), may hold values from -0.09375 to 0.09375
- down_weight: bfloat16 [18432, 4608], P(('tensor', 'draw'), 'batch'), may hold values from -0.046875 to 0.046875
- gate_up_noise: bfloat16 [4, 2, 4608, 18432], P('draw', None, 'batch', 'tensor'), may hold values from -1 to 1
- down_noise: bfloat16 [4, 18432, 4608], P('draw', 'tensor', 'batch'), may hold values from -1 to 1
- gate_up_left: bfloat16 [2, 4608, 64], P(None, 'batch'), may hold values from -0.09375 to 0.09375
- gate_up_right: bfloat16 [2, 64, 18432], P(None, None, 'tensor'), may hold values from -0.75 to 0.75
- down_left: bfloat16 [18432, 64], P('tensor'), may hold values from -0.046875 to 0.046875
- down_right: bfloat16 [64, 4608], P(None, 'batch'), may hold values from -0.75 to 0.75
Outputs:
- layer_out: bfloat16 [4, 512, 4608], P('draw', None, ('batch', 'tensor'))
- input_grad: bfloat16 [4, 512, 4608], P('draw', None, ('batch', 'tensor'))
- grad_gate_up_left: bfloat16 [2, 4608, 64], P(None, 'batch')
- grad_gate_up_right: bfloat16 [2, 64, 18432], P(None, None, 'tensor')
- grad_down_left: bfloat16 [18432, 64], P('tensor')
- grad_down_right: bfloat16 [64, 4608], P(None, 'batch')
All inputs are finite; a program needn't handle non-finite values.
Results may differ from a plain program's by a relative error of at most 0.029.
Values may be sent and summed in bfloat16 or wider, within the bound.
A program may use at most 128 MiB of HBM per device.

v0:
```python
import jax
import jax.numpy as jnp
from jax import lax
from jax.sharding import PartitionSpec as P

noise_sigma = 0.5
root_coeff = 0.7978845608028654
cubic_coeff = 0.044715


def gelu_pair(value):
    inner = root_coeff * (value + cubic_coeff * value * value * value)
    bend = jnp.tanh(inner)
    result = 0.5 * value * (1.0 + bend)
    slope = 0.5 * (1.0 + bend) + 0.5 * value * (1.0 - bend * bend) * root_coeff * (
        1.0 + 3.0 * cubic_coeff * value * value
    )
    return (result, slope)


def perturb(weight, noise):
    return (weight.astype(jnp.float32) * (1.0 + noise_sigma * noise.astype(jnp.float32))).astype(
        jnp.bfloat16
    )


def highest(left, right):
    return jnp.dot(left, right, precision=lax.Precision.HIGHEST, preferred_element_type=jnp.float32)


def on_device(
    tokens,
    cotangent,
    gate_up_weight,
    down_weight,
    gate_up_noise,
    down_noise,
    gate_up_left,
    gate_up_right,
    down_left,
    down_right,
):
    noise_gu = gate_up_noise[0]
    noise_dn = down_noise[0]
    rows_all = lax.all_gather(tokens[0], "tensor", axis=1, tiled=True)
    total_tokens = rows_all.shape[0]
    scale_grad = (lax.axis_size("draw") * total_tokens) ** (-0.5)
    right_gate = gate_up_right.astype(jnp.float32)
    left_gate = gate_up_left.astype(jnp.float32)
    down_left_f = down_left.astype(jnp.float32)
    down_right_f = down_right.astype(jnp.float32)
    noisy_gu = perturb(lax.all_gather(gate_up_weight, "draw", axis=2, tiled=True), noise_gu)
    noisy_dn = perturb(lax.all_gather(down_weight, "draw", axis=0, tiled=True), noise_dn)
    direct_gu = jnp.einsum("td,kdc->ktc", rows_all, noisy_gu, preferred_element_type=jnp.float32)
    low_part = jnp.einsum("td,kdr->ktr", rows_all, gate_up_left, preferred_element_type=jnp.float32)
    pre_part = direct_gu + jnp.einsum(
        "ktr,krc->ktc",
        low_part,
        right_gate,
        precision=lax.Precision.HIGHEST,
        preferred_element_type=jnp.float32,
    )
    pre = lax.psum_scatter(pre_part, "batch", scatter_dimension=1, tiled=True)
    active, slope = gelu_pair(pre[0])
    hidden = (active * pre[1]).astype(jnp.bfloat16)
    hidden_all = lax.all_gather(hidden, "batch", axis=0, tiled=True)
    low_down_part = jnp.dot(hidden_all, down_left, preferred_element_type=jnp.float32)
    direct_dn = jnp.dot(hidden_all, noisy_dn, preferred_element_type=jnp.float32)
    out_part = direct_dn + highest(low_down_part, down_right_f)
    layer_out = lax.psum_scatter(
        out_part.astype(jnp.bfloat16), "tensor", scatter_dimension=1, tiled=True
    )
    cot_all = lax.all_gather(cotangent[0], "tensor", axis=1, tiled=True)
    back_low_part = jnp.einsum("td,rd->tr", cot_all, down_right, preferred_element_type=jnp.float32)
    direct_hid = jnp.einsum("td,cd->tc", cot_all, noisy_dn, preferred_element_type=jnp.float32)
    hid_part = direct_hid + highest(back_low_part, down_left_f.T)
    hidden_grad = lax.psum_scatter(
        hid_part.astype(jnp.bfloat16), "batch", scatter_dimension=0, tiled=True
    ).astype(jnp.float32)
    grad_gate = (hidden_grad * pre[1] * slope).astype(jnp.bfloat16)
    grad_up = (hidden_grad * active).astype(jnp.bfloat16)
    pre_grad = jnp.stack([grad_gate, grad_up])
    pre_grad_all = lax.all_gather(pre_grad, "batch", axis=1, tiled=True)
    rank_part = jnp.einsum(
        "ktc,krc->ktr", pre_grad_all, gate_up_right, preferred_element_type=jnp.float32
    )
    direct_in = jnp.einsum(
        "ktc,kdc->td", pre_grad_all, noisy_gu, preferred_element_type=jnp.float32
    )
    in_part = direct_in + jnp.einsum(
        "ktr,kdr->td",
        rank_part,
        left_gate,
        precision=lax.Precision.HIGHEST,
        preferred_element_type=jnp.float32,
    )
    input_grad = lax.psum_scatter(
        in_part.astype(jnp.bfloat16), "tensor", scatter_dimension=1, tiled=True
    )
    rows_f = rows_all.astype(jnp.float32)
    left_term = jnp.einsum(
        "td,ktr->kdr",
        rows_f,
        rank_part,
        precision=lax.Precision.HIGHEST,
        preferred_element_type=jnp.float32,
    )
    down_right_term = highest(low_down_part.T, cot_all.astype(jnp.float32))
    right_term = jnp.einsum(
        "ktr,ktc->krc",
        low_part,
        pre_grad_all.astype(jnp.float32),
        precision=lax.Precision.HIGHEST,
        preferred_element_type=jnp.float32,
    )
    down_left_term = highest(hidden_all.astype(jnp.float32).T, back_low_part)
    left_sum, down_right_sum = lax.psum((left_term, down_right_term), ("tensor", "draw"))
    right_sum, down_left_sum = (
        lax.psum(right_term.astype(jnp.bfloat16), ("draw", "batch")).astype(jnp.float32),
        lax.psum(down_left_term.astype(jnp.bfloat16), ("draw", "batch")).astype(jnp.float32),
    )
    return (
        layer_out[None],
        input_grad[None],
        (scale_grad * left_sum).astype(jnp.bfloat16),
        (scale_grad * right_sum).astype(jnp.bfloat16),
        (scale_grad * down_left_sum).astype(jnp.bfloat16),
        (scale_grad * down_right_sum).astype(jnp.bfloat16),
    )


def solution(mesh):
    in_specs = (
        P("draw", None, ("batch", "tensor")),
        P("draw", None, ("batch", "tensor")),
        P(None, "batch", ("tensor", "draw")),
        P(("tensor", "draw"), "batch"),
        P("draw", None, "batch", "tensor"),
        P("draw", "tensor", "batch"),
        P(None, "batch", None),
        P(None, None, "tensor"),
        P("tensor", None),
        P(None, "batch"),
    )
    out_specs = (
        P("draw", None, ("batch", "tensor")),
        P("draw", None, ("batch", "tensor")),
        P(None, "batch", None),
        P(None, None, "tensor"),
        P("tensor", None),
        P(None, "batch"),
    )
    return jax.shard_map(
        on_device, mesh=mesh, in_specs=in_specs, out_specs=out_specs, check_vma=False
    )
```

profile of v0, /device:TPU:32, one launch (start us, length us, event | category | flops | bytes accessed | tf_op | source)
XLA Modules:
  0.0 1298.5 jit_solution(9534499755215904939)
XLA Ops:
  7.2 0.7 all-gather.19.cloned.1.call-update
  8.0 0.7 all-gather.13.cloned.1.call-update
  8.7 0.7 all-gather.17.cloned.1.call-update
  9.5 3.4 copy.34
  12.9 0.0 reduce-scatter.13.cloned.1.call-start
  13.0 68.2 %all-gather.19.cloned.1.call-done = bf16[1,512,1152]{1,2,0:T(8,128)(2,1)} async-done(((bf16[1,512,72]{1,2,0:T(8,128)(2,1)}), bf16[1,512,1152]{1,2,0:T(8,128)(2,1)}) %all-gather.19.cloned.1.call-update) | async-done | bytes 1179664 | tf_op jit(solution)/shard_map/all_gather | solution.py:73
  81.2 1.6 fusion.13
  82.8 36.6 %all-gather.13.cloned.1.call-done = bf16[1152,1152]{1,0:T(8,128)(2,1)} async-done(((bf16[288,1152]{1,0:T(8,128)(2,1)}), bf16[1152,1152]{1,0:T(8,128)(2,1)}) %all-gather.13.cloned.1.call-update) | async-done | bytes 2654224 | tf_op jit(solution)/shard_map/all_gather | solution.py:53
  119.4 4.6 convolution_bitcast_fusion.2
  124.0 1.2 fusion.4
  125.2 1.4 copy.49
  126.6 0.0 reduce-scatter.7.cloned.1.call-start
  126.7 63.4 %all-gather.17.cloned.1.call-done = bf16[1,512,1152]{1,2,0:T(8,128)(2,1)} async-done(((bf16[1,512,72]{1,2,0:T(8,128)(2,1)}), bf16[1,512,1152]{1,2,0:T(8,128)(2,1)}) %all-gather.17.cloned.1.call-update) | async-done | bytes 1179664 | tf_op jit(solution)/shard_map/all_gather | solution.py:45
  190.1 1.6 fusion.7
  191.8 58.5 %all-gather.9.cloned.1.call-done = bf16[2,1152,1152]{1,0,2:T(2,128)(2,1)} async-done(((bf16[2,1152,288]{1,0,2:T(2,128)(2,1)}), bf16[2,1152,1152]{1,0,2:T(2,128)(2,1)}) %all-gather.9.cloned.1.call-update) | async-done | bytes 5308432 | tf_op jit(solution)/shard_map/all_gather | solution.py:52
  250.2 16.5 %copy.35 = bf16[2,1152,1152]{2,1,0:T(8,128)(2,1)} copy(bf16[2,1152,1152]{1,0,2:T(2,128)(2,1)} %all-gather.9.cloned.1.call-done) | data formatting | bytes 10616832 | tf_op jit(solution)/shard_map/all_gather | solution.py:52
  266.7 6.2 fusion.9
  272.9 4.3 convolution_add_fusion
  277.2 0.0 all-gather.11.cloned.1.call-start
  277.2 14.0 %reduce-scatter.13.cloned.1.call-done = bf16[128,1152]{1,0:T(8,128)(2,1)} async-done(((bf16[512,1152]{1,0:T(8,128)(2,1)}), bf16[128,1152]{1,0:T(8,128)(2,1)}) %reduce-scatter.13.cloned.1.call-update) | async-done | bytes 294928
  291.3 1.2 copy.50
  292.4 61.1 %reduce-scatter.7.cloned.1.call-done = f32[2,128,1152]{1,2,0:T(8,128)} async-done(((f32[2,512,1152]{1,2,0:T(8,128)}), f32[2,128,1152]{1,2,0:T(8,128)}) %reduce-scatter.7.cloned.1.call-update) | async-done | bytes 1179664 | tf_op jit(solution)/shard_map/reduce_scatter | solution.py:63
  353.5 2.5 fusion.30
  356.1 0.9 pad_maximum_fusion
  357.0 0.2 all-reduce.7.cloned.1.call-start
  357.2 22.6 %all-gather.11.cloned.1.call-done = bf16[512,1152]{0,1:T(8,128)(2,1)} async-done(((bf16[128,1152]{0,1:T(8,128)(2,1)}), bf16[512,1152]{0,1:T(8,128)(2,1)}) %all-gather.11.cloned.1.call-update) | async-done | bytes 1179664 | tf_op jit(solution)/shard_map/all_gather | solution.py:66
  379.8 1.6 fusion.39
  381.4 3.1 convolution_convert_fusion.1
  384.5 1.9 fusion.11
  386.4 25.6 %all-gather.15.cloned.1.call-done = bf16[2,512,1152]{1,2,0:T(8,128)(2,1)} async-done(((bf16[2,128,1152]{1,2,0:T(8,128)(2,1)}), bf16[2,512,1152]{1,2,0:T(8,128)(2,1)}) %all-gather.15.cloned.1.call-update) | async-done | bytes 2359312 | tf_op jit(solution)/shard_map/all_gather | solution.py:83
  412.0 4.7 convolution_convert_fusion
  416.8 0.0 all-reduce.5.cloned.1.call-start
  416.9 0.5 fusion.40
  417.4 0.7 copy-done.4
  418.1 2.1 convolution_bitcast_fusion.3
  420.3 4.7 fusion.27
  425.0 2.3 fusion.3
  427.3 0.0 reduce-scatter.11.cloned.1.call-start
  427.3 5.7 convolution_bitcast_fusion.1
  433.0 2.3 fusion.5
  435.3 121.7 %all-reduce.7.cloned.1.call-done = (bf16[2,64,1152]{2,1,0:T(8,128)(2,1)}, bf16[1152,64]{0,1:T(8,128)(2,1)}) async-done(((bf16[2,64,1152]{2,1,0:T(8,128)(2,1)}, bf16[1152,64]{0,1:T(8,128)(2,1)}), (bf16[2,64,1152]{2,1,0:T(8,128)(2,1)}, bf16[1152,64]{0,1:T(8,128)(2,1)})) %all-reduce.7.cloned.1.call-update) | async-done | bytes 442384 | tf_op jit(solution)/shard_map/psum | solution.py:119
  557.0 1.6 multiply_convert_fusion.4
  558.6 1.7 multiply_convert_fusion
  560.4 586.7 %all-reduce.5.cloned.1.call-done = (f32[2,1152,64]{1,2,0:T(8,128)}, f32[64,1152]{1,0:T(8,128)}) async-done(((f32[2,1152,64]{1,2,0:T(8,128)}, f32[64,1152]{1,0:T(8,128)}), (f32[2,1152,64]{1,2,0:T(8,128)}, f32[64,1152]{1,0:T(8,128)})) %all-reduce.5.cloned.1.call-update) | async-done | bytes 884752 | tf_op jit(solution)/shard_map/psum | solution.py:117
  1147.1 1.6 multiply_convert_fusion.3
  1148.7 1.8 multiply_convert_fusion.1
  1150.6 70.1 %reduce-scatter.9.cloned.1.call-done = bf16[512,72]{0,1:T(8,128)(2,1)} async-done(((bf16[512,1152]{0,1:T(8,128)(2,1)}), bf16[512,72]{0,1:T(8,128)(2,1)}) %reduce-scatter.9.cloned.1.call-update) | async-done | bytes 73744 | tf_op jit(solution)/shard_map/reduce_scatter | solution.py:70
  1220.7 70.9 %reduce-scatter.11.cloned.1.call-done = bf16[512,72]{0,1:T(8,128)(2,1)} async-done(((bf16[512,1152]{0,1:T(8,128)(2,1)}), bf16[512,72]{0,1:T(8,128)(2,1)}) %reduce-scatter.11.cloned.1.call-update) | async-done | bytes 73744 | tf_op jit(solution)/shard_map/reduce_scatter | solution.py:97
  (30 shorter events, 0.4 us)
Async XLA Ops:
  7.2 265.7 %copy-start = (bf16[2,64,1152]{2,1,0:T(8,128)(2,1)S(1)}, bf16[2,64,1152]{2,1,0:T(8,128)(2,1)}, u32[]{:S(2)}) copy-start(bf16[2,64,1152]{2,1,0:T(8,128)(2,1)} %param.17) | copy-start | bytes 884740
  7.2 74.0 %all-gather.19.cloned.1.call-start = ((), (), s32[]{:S(2)}) async-start(), calls=%async_computation.12 | async-start | bytes 1253376 | tf_op jit(solution)/shard_map/all_gather | solution.py:73
  7.9 73.3 %copy-start.7 = (bf16[64,1152]{1,0:T(8,128)(2,1)S(1)}, bf16[64,1152]{1,0:T(8,128)(2,1)}, u32[]{:S(2)}) copy-start(bf16[64,1152]{1,0:T(8,128)(2,1)} %param.19) | copy-start | bytes 442372
  7.9 111.5 %all-gather.13.cloned.1.call-start = ((), (), s32[]{:S(2)}) async-start(), calls=%async_computation.7 | async-start | bytes 3317760 | tf_op jit(solution)/shard_map/all_gather | solution.py:53
  8.7 181.5 %all-gather.17.cloned.1.call-start = ((), (), s32[]{:S(2)}) async-start(), calls=%async_computation.11 | async-start | bytes 1253376 | tf_op jit(solution)/shard_map/all_gather | solution.py:45
  9.4 240.8 %all-gather.9.cloned.1.call-start = ((), (), s32[]{:S(2)}) async-start(), calls=%async_computation.4 | async-start | bytes 6635520 | tf_op jit(solution)/shard_map/all_gather | solution.py:52
  12.9 278.3 %reduce-scatter.13.cloned.1.call-start = ((), (), s32[]{:S(2)}) async-start(), calls=%async_computation.13 | async-start | bytes 1474560
  82.8 41.2 %copy-start.6 = (bf16[1152,64]{0,1:T(8,128)(2,1)S(1)}, bf16[1152,64]{0,1:T(8,128)(2,1)}, u32[]{:S(2)}) copy-start(bf16[1152,64]{0,1:T(8,128)(2,1)} %param.18) | copy-start | bytes 442372
  125.2 64.9 %copy-start.5 = (bf16[2,1152,64]{1,2,0:T(8,128)(2,1)S(1)}, bf16[2,1152,64]{1,2,0:T(8,128)(2,1)}, u32[]{:S(2)}) copy-start(bf16[2,1152,64]{1,2,0:T(8,128)(2,1)} %param.16) | copy-start | bytes 884740
  126.6 226.9 %reduce-scatter.7.cloned.1.call-start = ((), (), s32[]{:S(2)}) async-start(), calls=%async_computation.5 | async-start | bytes 5898240 | tf_op jit(solution)/shard_map/reduce_scatter | solution.py:63
  191.7 75.0 %copy-start.3 = (bf16[1,512,1152]{1,2,0:T(8,128)(2,1)S(1)}, bf16[1,512,1152]{1,2,0:T(8,128)(2,1)}, u32[]{:S(2)}) copy-start(bf16[1,512,1152]{1,2,0:T(8,128)(2,1)} %all-gather.17.cloned.1.call-done) | copy-start | bytes 3538948
  277.2 102.6 %all-gather.11.cloned.1.call-start = ((), (), s32[]{:S(2)}) async-start(), calls=%async_computation.6 | async-start | bytes 1474560 | tf_op jit(solution)/shard_map/all_gather | solution.py:66
  356.0 28.5 %copy-start.2 = (bf16[1,512,1152]{1,2,0:T(8,128)(2,1)S(1)}, bf16[1,512,1152]{1,2,0:T(8,128)(2,1)}, u32[]{:S(2)}) copy-start(bf16[1,512,1152]{1,2,0:T(8,128)(2,1)} %all-gather.19.cloned.1.call-done) | copy-start | bytes 3538948
  356.0 56.0 %all-gather.15.cloned.1.call-start = ((), (), s32[]{:S(2)}) async-start(), calls=%async_computation.9 | async-start | bytes 2949120 | tf_op jit(solution)/shard_map/all_gather | solution.py:83
  357.0 200.1 %all-reduce.7.cloned.1.call-start = ((), (), s32[]{:S(2)}) async-start(), calls=%async_computation.15 | async-start | bytes 884736 | tf_op jit(solution)/shard_map/psum | solution.py:119
  412.0 4.8 copy-start.1
  416.8 730.3 %all-reduce.5.cloned.1.call-start = ((), (), s32[]{:S(2)}) async-start(), calls=%async_computation.14 | async-start | bytes 1769472 | tf_op jit(solution)/shard_map/psum | solution.py:117
  416.9 1.3 copy-start.4
  420.3 800.4 %reduce-scatter.9.cloned.1.call-start = ((), (), s32[]{:S(2)}) async-start(), calls=%async_computation.8 | async-start | bytes 1253376 | tf_op jit(solution)/shard_map/reduce_scatter | solution.py:70
  427.3 864.4 %reduce-scatter.11.cloned.1.call-start = ((), (), s32[]{:S(2)}) async-start(), calls=%async_computation.10 | async-start | bytes 1253376 | tf_op jit(solution)/shard_map/reduce_scatter | solution.py:97
Sparse Core Ops, SparseCore 0:
  9.8 71.3 all-gather.18
  83.0 36.3 all-gather.12
  121.2 68.8 all-gather.16
  191.8 58.4 all-gather.8
  252.9 38.3 reduce-scatter.12
  294.1 59.3 reduce-scatter.6
  356.1 23.6 all-gather.10
  381.6 30.3 all-gather.14
  416.9 140.0 all-reduce.6
  560.4 586.6 all-reduce.4
  1150.2 70.4 reduce-scatter.8
  1223.6 67.9 reduce-scatter.10
where the time goes:
time: 1300 us
  waiting for transfers between devices  1200 us (92%)
  matrix products  48.3 us (4%)
  local copies, waits for them, and re-layouts  23.2 us (2%)
  between operations  14.4 us (1%)
    psum x1, waiting for transfers between devices, on_device(): lax.psum((left_term, down_right_term), ('tensor', 'draw'))  587 us
    psum x1, waiting for transfers between devices, on_device(): lax.psum(right_term.astype(jnp.bfloat16), ('draw', 'batch'))  122 us
    reduce_scatter x1, waiting for transfers between devices, on_device(): lax.psum_scatter(in_part.astype(jnp.bfloat16), 'tensor', scatter_dimensio...  70.9 us
    reduce_scatter x1, waiting for transfers between devices, on_device(): lax.psum_scatter(out_part.astype(jnp.bfloat16), 'tensor', scatter_dimensi...  70.1 us
    all_gather x1, waiting for transfers between devices, on_device(): cot_all = lax.all_gather(cotangent[0], 'tensor', axis=1, tiled=True)  68.2 us
    all_gather x1, waiting for transfers between devices, on_device(): rows_all = lax.all_gather(tokens[0], 'tensor', axis=1, tiled=True)  63.4 us
    reduce_scatter x1, waiting for transfers between devices, on_device(): pre = lax.psum_scatter(pre_part, 'batch', scatter_dimension=1, tiled=True)  61.1 us
    all_gather x1, waiting for transfers between devices, on_device(): lax.all_gather(gate_up_weight, 'draw', axis=2, tiled=True)  58.5 us
  transfers between devices with their start and end apart: 12, of which 12 were waited for; matrix products, arithmetic and copies ran while one was open for 6% of the time, Pallas kernels for 0%

commit v1 on v0

--- a/solution.py
+++ b/solution.py
@@ -60,16 +60,15 @@
         precision=lax.Precision.HIGHEST,
         preferred_element_type=jnp.float32,
     )
-    pre = lax.psum_scatter(pre_part, "batch", scatter_dimension=1, tiled=True)
+    pre = lax.psum_scatter(
+        pre_part.astype(jnp.bfloat16), "batch", scatter_dimension=1, tiled=True
+    ).astype(jnp.float32)
     active, slope = gelu_pair(pre[0])
     hidden = (active * pre[1]).astype(jnp.bfloat16)
     hidden_all = lax.all_gather(hidden, "batch", axis=0, tiled=True)
     low_down_part = jnp.dot(hidden_all, down_left, preferred_element_type=jnp.float32)
     direct_dn = jnp.dot(hidden_all, noisy_dn, preferred_element_type=jnp.float32)
     out_part = direct_dn + highest(low_down_part, down_right_f)
-    layer_out = lax.psum_scatter(
-        out_part.astype(jnp.bfloat16), "tensor", scatter_dimension=1, tiled=True
-    )
     cot_all = lax.all_gather(cotangent[0], "tensor", axis=1, tiled=True)
     back_low_part = jnp.einsum("td,rd->tr", cot_all, down_right, preferred_element_type=jnp.float32)
     direct_hid = jnp.einsum("td,cd->tc", cot_all, noisy_dn, preferred_element_type=jnp.float32)
@@ -94,14 +93,11 @@
         precision=lax.Precision.HIGHEST,
         preferred_element_type=jnp.float32,
     )
-    input_grad = lax.psum_scatter(
-        in_part.astype(jnp.bfloat16), "tensor", scatter_dimension=1, tiled=True
-    )
     rows_f = rows_all.astype(jnp.float32)
     left_term = jnp.einsum(
-        "td,ktr->kdr",
+        "ktr,td->krd",
+        rank_part,
         rows_f,
-        rank_part,
         precision=lax.Precision.HIGHEST,
         preferred_element_type=jnp.float32,
     )
@@ -113,19 +109,39 @@
         precision=lax.Precision.HIGHEST,
         preferred_element_type=jnp.float32,
     )
-    down_left_term = highest(hidden_all.astype(jnp.float32).T, back_low_part)
-    left_sum, down_right_sum = lax.psum((left_term, down_right_term), ("tensor", "draw"))
-    right_sum, down_left_sum = (
-        lax.psum(right_term.astype(jnp.bfloat16), ("draw", "batch")).astype(jnp.float32),
-        lax.psum(down_left_term.astype(jnp.bfloat16), ("draw", "batch")).astype(jnp.float32),
+    down_left_term = highest(back_low_part.T, hidden_all.astype(jnp.float32))
+    rank = right_term.shape[1]
+    width = out_part.shape[1]
+    by_feature = jnp.concatenate(
+        [out_part, in_part, left_term.reshape(2 * rank, width), down_right_term]
+    ).astype(jnp.bfloat16)
+    mine = lax.psum_scatter(by_feature.T, "tensor", scatter_dimension=0, tiled=True)
+    layer_out = mine[:, :total_tokens].T
+    input_grad = mine[:, total_tokens : 2 * total_tokens].T
+    feature_sums = lax.psum(mine[:, 2 * total_tokens :], "draw")
+    feature_sums = lax.all_gather(
+        (scale_grad * feature_sums.astype(jnp.float32)).astype(jnp.bfloat16),
+        "tensor",
+        axis=0,
+        tiled=True,
+    ).T
+    by_hidden = jnp.concatenate([right_term.reshape(2 * rank, -1), down_left_term])
+    by_hidden = lax.psum_scatter(
+        by_hidden.astype(jnp.bfloat16).T, ("draw", "batch"), scatter_dimension=0, tiled=True
     )
+    hidden_sums = lax.all_gather(
+        (scale_grad * by_hidden.astype(jnp.float32)).astype(jnp.bfloat16),
+        ("draw", "batch"),
+        axis=0,
+        tiled=True,
+    ).T
     return (
         layer_out[None],
         input_grad[None],
-        (scale_grad * left_sum).astype(jnp.bfloat16),
-        (scale_grad * right_sum).astype(jnp.bfloat16),
-        (scale_grad * down_left_sum).astype(jnp.bfloat16),
-        (scale_grad * down_right_sum).astype(jnp.bfloat16),
+        jnp.swapaxes(feature_sums[: 2 * rank].reshape(2, rank, width), 1, 2),
+        hidden_sums[: 2 * rank].reshape(2, rank, -1),
+        hidden_sums[2 * rank :].T,
+        feature_sums[2 * rank :],
     )
 
 

time: 1300 us -> 615 us (0.47)
  waiting for transfers between devices: 1200 us -> 425 us
  blocking collectives: 0 us -> 75.4 us
  local copies, waits for them, and re-layouts: 23.2 us -> 42.1 us
    psum x2 -> x0, waiting for transfers between devices: 708 us -> none  [the longest x1 587 us: on_device(): lax.psum((left_term, down_right_term), ('tensor', 'draw'))]
    reduce_scatter x3, waiting for transfers between devices: 202 us -> 140 us  [the longest x1 50.7 us: on_device(): lax.psum_scatter(by_feature.T, 'tensor', scatter_dimension=0, tiled=True)]
    all_gather x0 -> x2, blocking collectives: none -> 58.3 us  [the longest x1 35.1 us: on_device(): lax.all_gather((scale_grad * feature_sums.astype(jnp.float32)).astype(jnp...]
    all_gather x1, waiting for transfers between devices: 68.2 us -> 36.5 us  [on_device(): cot_all = lax.all_gather(cotangent[0], 'tensor', axis=1, tiled=True)]
    unnamed x13 -> x11, waiting for transfers between devices: 16.2 us -> 42.6 us
    psum x0 -> x1, blocking collectives: none -> 17.1 us  [on_device(): feature_sums = lax.psum(mine[:, 2 * total_tokens:], 'draw')]
    unnamed x19 -> x37, local copies, waits for them, and re-layouts: 6.77 us -> 21.5 us
  transfers between devices with their start and end apart: 12 -> 10, of which waited for: 12 -> 10; matrix products, arithmetic and copies ran while one was open for 6% -> 14% of each run, Pallas kernels for 0% -> 0%
where the time goes in v1:
time: 615 us; the launch traced here: 613 us
  waiting for transfers between devices  425 us (69%)
  blocking collectives  75.4 us (12%)
  matrix products  44.4 us (7%)
  local copies, waits for them, and re-layouts  42.1 us (7%)
  between operations  14.5 us (2%)
  other arithmetic  11.2 us (2%)
    all_gather x1, waiting for transfers between devices, on_device(): rows_all = lax.all_gather(tokens[0], 'tensor', axis=1, tiled=True)  68.4 us
    all_gather x1, waiting for transfers between devices, on_device(): lax.all_gather(gate_up_weight, 'draw', axis=2, tiled=True)  58.6 us
    reduce_scatter x1, waiting for transfers between devices, on_device(): lax.psum_scatter(by_feature.T, 'tensor', scatter_dimension=0, tiled=True)  50.7 us
    reduce_scatter x1, waiting for transfers between devices, on_device(): lax.psum_scatter(by_hidden.astype(jnp.bfloat16).T, ('draw', 'batch'), sca...  50.7 us
    unnamed x11, waiting for transfers between devices  42.6 us
    reduce_scatter x1, waiting for transfers between devices, on_device(): lax.psum_scatter(hid_part.astype(jnp.bfloat16), 'batch', scatter_dimensio...  38.2 us
    all_gather x1, waiting for transfers between devices, on_device(): cot_all = lax.all_gather(cotangent[0], 'tensor', axis=1, tiled=True)  36.5 us
    all_gather x1, waiting for transfers between devices, on_device(): lax.all_gather(down_weight, 'draw', axis=0, tiled=True)  36.4 us
  transfers between devices with their start and end apart: 10, of which 10 were waited for; matrix products, arithmetic and copies ran while one was open for 14% of the time, Pallas kernels for 0%

profile of v1, /device:TPU:32, one launch (start us, length us, event | category | flops | bytes accessed | tf_op | source)
XLA Modules:
  0.0 612.8 jit_solution(14783164072205787213)
XLA Ops:
  8.0 3.4 copy.58
  11.5 0.7 all-gather.19.cloned.1.call-update
  12.8 68.4 %all-gather.17.cloned.1.call-done = bf16[1,512,1152]{1,2,0:T(8,128)(2,1)} async-done(((bf16[1,512,72]{1,2,0:T(8,128)(2,1)}), bf16[1,512,1152]{1,2,0:T(8,128)(2,1)}) %all-gather.17.cloned.1.call-update) | async-done | bytes 1179664 | tf_op jit(solution)/shard_map/all_gather | solution.py:45
  81.2 1.6 fusion.8
  82.8 58.6 %all-gather.9.cloned.1.call-done = bf16[2,1152,1152]{1,0,2:T(2,128)(2,1)} async-done(((bf16[2,1152,288]{1,0,2:T(2,128)(2,1)}), bf16[2,1152,1152]{1,0,2:T(2,128)(2,1)}) %all-gather.9.cloned.1.call-update) | async-done | bytes 5308432 | tf_op jit(solution)/shard_map/all_gather | solution.py:52
  141.5 16.4 %copy.59 = bf16[2,1152,1152]{2,1,0:T(8,128)(2,1)} copy(bf16[2,1152,1152]{1,0,2:T(2,128)(2,1)} %all-gather.9.cloned.1.call-done) | data formatting | bytes 10616832 | tf_op jit(solution)/shard_map/all_gather | solution.py:52
  157.9 6.1 fusion.10
  164.0 3.8 fusion.2
  167.8 6.5 %copy.75 = bf16[2,512,1152]{2,0,1:T(2,128)(2,1)S(1)} copy(bf16[2,512,1152]{1,2,0:T(8,128)(2,1)} %fusion.2) | data formatting | bytes 4718592
  174.3 1.8 copy.86
  176.1 36.5 %all-gather.19.cloned.1.call-done = bf16[1,512,1152]{1,2,0:T(8,128)(2,1)} async-done(((bf16[1,512,72]{1,2,0:T(8,128)(2,1)}), bf16[1,512,1152]{1,2,0:T(8,128)(2,1)}) %all-gather.19.cloned.1.call-update) | async-done | bytes 1179664 | tf_op jit(solution)/shard_map/all_gather | solution.py:72
  212.6 1.6 fusion.13
  214.2 36.4 %all-gather.13.cloned.1.call-done = bf16[1152,1152]{1,0:T(8,128)(2,1)} async-done(((bf16[288,1152]{1,0:T(8,128)(2,1)}), bf16[1152,1152]{1,0:T(8,128)(2,1)}) %all-gather.13.cloned.1.call-update) | async-done | bytes 2654224 | tf_op jit(solution)/shard_map/all_gather | solution.py:53
  250.6 4.6 convolution_bitcast_fusion.2
  255.2 1.2 fusion.5
  256.4 1.5 copy.77
  258.0 40.6 %reduce-scatter.13.cloned.1.call-done = bf16[128,2304]{1,0:T(8,128)(2,1)} async-done(((bf16[512,2304]{1,0:T(8,128)(2,1)}), bf16[128,2304]{1,0:T(8,128)(2,1)}) %reduce-scatter.13.cloned.1.call-update) | async-done | bytes 589840
  298.6 1.9 reshape.46
  300.5 38.2 %reduce-scatter.15.cloned.1.call-done = bf16[128,1152]{1,0:T(8,128)(2,1)} async-done(((bf16[512,1152]{1,0:T(8,128)(2,1)}), bf16[128,1152]{1,0:T(8,128)(2,1)}) %reduce-scatter.15.cloned.1.call-update) | async-done | bytes 294928 | tf_op jit(solution)/shard_map/reduce_scatter | solution.py:76
  338.7 2.2 fusion.30
  341.0 0.9 pad_maximum_fusion
  342.1 22.5 %all-gather.11.cloned.1.call-done = bf16[512,1152]{1,0:T(8,128)(2,1)} async-done(((bf16[128,1152]{1,0:T(8,128)(2,1)}), bf16[512,1152]{1,0:T(8,128)(2,1)}) %all-gather.11.cloned.1.call-update) | async-done | bytes 1179664 | tf_op jit(solution)/shard_map/all_gather | solution.py:68
  364.7 1.9 fusion.40
  366.6 2.6 convolution_convert_fusion.2
  369.2 1.2 convolution_convert_fusion.3
  370.4 3.7 fusion.27
  374.2 2.3 fusion.4
  376.5 20.1 %all-gather.15.cloned.1.call-done = bf16[2,512,1152]{2,1,0:T(8,128)(2,1)} async-done(((bf16[2,128,1152]{2,1,0:T(8,128)(2,1)}), bf16[2,512,1152]{2,1,0:T(8,128)(2,1)}) %all-gather.15.cloned.1.call-update) | async-done | bytes 2359312 | tf_op jit(solution)/shard_map/all_gather | solution.py:82
  396.6 3.1 convolution_convert_fusion
  399.7 0.9 maximum_bitcast_fusion.1
  400.7 1.1 copy.81
  401.8 0.8 fusion.41
  402.7 7.4 %convolution_bitcast_fusion.1 = f32[512,1152]{1,0:T(8,128)S(1)} fusion(bf16[2,512,1152]{2,1,0:T(8,128)(2,1)S(1)} %copy-done.1, bf16[1,2,1152,1152]{3,2,1,0:T(8,128)(2,1)} %param.14, bf16[2,1152,1152]{2,1,0:T(8,128)(2,1)} %copy.59), kind=kOutput, calls=%fused_computation.10 | convolution fusion | flops 2733834240 | bytes 15335424 | tf_op jit(solution)/shard_map/ktc,kdc->td/dot_general | solution.py:86
  410.1 1.2 fusion.6
  411.3 1.3 convolution_convert_fusion.1
  412.6 6.3 %maximum_bitcast_fusion = bf16[1152,1216]{0,1:T(8,128)(2,1)S(1)} fusion(bf16[64,1152]{1,0:T(8,128)(2,1)S(1)} %convolution_convert_fusion.3, bf16[128,1152]{1,0:T(8,128)(2,1)S(1)} %bitcast.131, bf16[512,1152]{1,0:T(8,128)(2,1)S(1)} %fusion.6, bf16[512,1152]{1,0:T(8,128)(2,1)S(1)} %copy-done.6), kind=kLoop, calls=%fused_computation.15 | loop fusion | flops 11206656 | bytes 5603328 | tf_op jit(solution)/shard_map/transpose | solution.py:118
  418.9 3.6 copy.79
  422.5 50.7 %reduce-scatter.19.cloned.1.call-done = bf16[72,192]{1,0:T(8,128)(2,1)} async-done(((bf16[1152,192]{1,0:T(8,128)(2,1)}), bf16[72,192]{1,0:T(8,128)(2,1)}) %reduce-scatter.19.cloned.1.call-update) | async-done | bytes 27664 | tf_op jit(solution)/shard_map/reduce_scatter | solution.py:129
  473.2 0.8 multiply_convert_fusion.1
  474.0 23.2 %all_gather.31 = bf16[1152,192]{1,0:T(8,128)(2,1)S(1)} all-gather(bf16[72,192]{1,0:T(8,128)(2,1)S(1)} %multiply_convert_fusion.1), channel_id=1, replica_groups=mesh['tensor'=16,'draw'=4,'batch'=4] {'draw','batch'}, dimensions={0}, use_global_device_ids=true | all-gather | bytes 470016 | tf_op jit(solution)/shard_map/all_gather | solution.py:132
  497.4 0.7 slice.43
  498.9 50.7 %reduce-scatter.17.cloned.1.call-done = bf16[72,1216]{1,0:T(8,128)(2,1)} async-done(((bf16[1152,1216]{1,0:T(8,128)(2,1)}), bf16[72,1216]{1,0:T(8,128)(2,1)}) %reduce-scatter.17.cloned.1.call-update) | async-done | bytes 175120 | tf_op jit(solution)/shard_map/reduce_scatter | solution.py:118
  549.5 0.8 slice.41
  550.4 17.1 %psum.7 = bf16[72,192]{1,0:T(8,128)(2,1)S(1)} all-reduce(bf16[72,192]{1,0:T(8,128)(2,1)S(1)} %slice.41), channel_id=1, replica_groups=mesh['tensor'=16,'draw'=4,'batch'=4] {'draw'}, use_global_device_ids=true, to_apply=%region_3.0 | all-reduce | flops 13824 | bytes 55296 | tf_op jit(solution)/shard_map/psum | solution.py:121
  567.5 35.1 %all_gather.30 = bf16[1152,192]{1,0:T(8,128)(2,1)S(1)} all-gather(bf16[72,192]{1,0:T(8,128)(2,1)S(1)} %multiply_convert_fusion.2), channel_id=1, replica_groups=mesh['tensor'=16,'draw'=4,'batch'=4] {'tensor'}, dimensions={0}, use_global_device_ids=true | all-gather | bytes 470016 | tf_op jit(solution)/shard_map/all_gather | solution.py:122
  602.8 0.7 slice.42
  604.4 0.7 copy.70
  605.2 0.7 copy.71
  (54 shorter events, 4.2 us)
Async XLA Ops:
  7.2 156.8 %copy-start = (bf16[2,64,1152]{2,1,0:T(8,128)(2,1)S(1)}, bf16[2,64,1152]{2,1,0:T(8,128)(2,1)}, u32[]{:S(2)}) copy-start(bf16[2,64,1152]{2,1,0:T(8,128)(2,1)} %param.17) | copy-start | bytes 884740
  7.2 74.0 %copy-start.7 = (bf16[2,1152,64]{1,2,0:T(8,128)(2,1)S(1)}, bf16[2,1152,64]{1,2,0:T(8,128)(2,1)}, u32[]{:S(2)}) copy-start(bf16[2,1152,64]{1,2,0:T(8,128)(2,1)} %param.16) | copy-start | bytes 884740
  7.2 74.0 %all-gather.17.cloned.1.call-start = ((), (), s32[]{:S(2)}) async-start(), calls=%async_computation.8 | async-start | bytes 1253376 | tf_op jit(solution)/shard_map/all_gather | solution.py:45
  7.9 133.5 %all-gather.9.cloned.1.call-start = ((), (), s32[]{:S(2)}) async-start(), calls=%async_computation.4 | async-start | bytes 6635520 | tf_op jit(solution)/shard_map/all_gather | solution.py:52
  11.4 201.2 %all-gather.19.cloned.1.call-start = ((), (), s32[]{:S(2)}) async-start(), calls=%async_computation.9 | async-start | bytes 1253376 | tf_op jit(solution)/shard_map/all_gather | solution.py:72
  12.2 238.5 %all-gather.13.cloned.1.call-start = ((), (), s32[]{:S(2)}) async-start(), calls=%async_computation.6 | async-start | bytes 3317760 | tf_op jit(solution)/shard_map/all_gather | solution.py:53
  12.7 285.8 %reduce-scatter.13.cloned.1.call-start = ((), (), s32[]{:S(2)}) async-start(), calls=%async_computation.10 | async-start | bytes 2949120
  82.8 75.1 %copy-start.4 = (bf16[1,512,1152]{1,2,0:T(8,128)(2,1)S(1)}, bf16[1,512,1152]{1,2,0:T(8,128)(2,1)}, u32[]{:S(2)}) copy-start(bf16[1,512,1152]{1,2,0:T(8,128)(2,1)} %all-gather.17.cloned.1.call-done) | copy-start | bytes 3538948
  174.3 38.3 %copy-start.9 = (bf16[64,1152]{1,0:T(8,128)(2,1)S(1)}, bf16[64,1152]{1,0:T(8,128)(2,1)}, u32[]{:S(2)}) copy-start(bf16[64,1152]{1,0:T(8,128)(2,1)} %param.19) | copy-start | bytes 442372
  176.1 162.7 %reduce-scatter.15.cloned.1.call-start = ((), (), s32[]{:S(2)}) async-start(), calls=%async_computation.11 | async-start | bytes 1474560 | tf_op jit(solution)/shard_map/reduce_scatter | solution.py:76
  214.2 41.0 %copy-start.8 = (bf16[1152,64]{0,1:T(8,128)(2,1)S(1)}, bf16[1152,64]{0,1:T(8,128)(2,1)}, u32[]{:S(2)}) copy-start(bf16[1152,64]{0,1:T(8,128)(2,1)} %param.18) | copy-start | bytes 442372
  257.9 106.7 %all-gather.11.cloned.1.call-start = ((), (), s32[]{:S(2)}) async-start(), calls=%async_computation.5 | async-start | bytes 1474560 | tf_op jit(solution)/shard_map/all_gather | solution.py:68
  340.9 28.3 %copy-start.2 = (bf16[1,512,1152]{1,2,0:T(8,128)(2,1)S(1)}, bf16[1,512,1152]{1,2,0:T(8,128)(2,1)}, u32[]{:S(2)}) copy-start(bf16[1,512,1152]{1,2,0:T(8,128)(2,1)} %all-gather.19.cloned.1.call-done) | copy-start | bytes 3538948
  341.0 55.7 %all-gather.15.cloned.1.call-start = ((), (), s32[]{:S(2)}) async-start(), calls=%async_computation.7 | async-start | bytes 2949120 | tf_op jit(solution)/shard_map/all_gather | solution.py:82
  341.9 131.3 %reduce-scatter.19.cloned.1.call-start = ((), (), s32[]{:S(2)}) async-start(), calls=%async_computation.13 | async-start | bytes 626688 | tf_op jit(solution)/shard_map/reduce_scatter | solution.py:129
  364.7 5.7 copy-start.3
  364.7 5.7 copy-start.12
  370.4 3.8 copy-start.10
  396.6 5.2 copy-start.1
  401.8 147.8 %reduce-scatter.17.cloned.1.call-start = ((), (), s32[]{:S(2)}) async-start(), calls=%async_computation.12 | async-start | bytes 3133440 | tf_op jit(solution)/shard_map/reduce_scatter | solution.py:118
  410.0 1.3 copy-start.5
  410.1 2.5 copy-start.6
  549.5 54.7 %copy-start.11 = (bf16[72,1216]{1,0:T(8,128)(2,1)S(1)}, bf16[72,1216]{1,0:T(8,128)(2,1)}, u32[]{:S(2)}) copy-start(bf16[72,1216]{1,0:T(8,128)(2,1)} %reduce-scatter.17.cloned.1.call-done) | copy-start | bytes 525316
Sparse Core Ops, SparseCore 0:
  9.8 71.3 all-gather.16
  83.0 58.4 all-gather.8
  143.3 69.2 all-gather.18
  214.3 36.3 all-gather.12
  253.3 45.2 reduce-scatter.12
  301.5 37.2 reduce-scatter.14
  341.1 23.4 all-gather.10
  366.5 30.0 all-gather.14
  401.9 71.2 reduce-scatter.18
  475.6 73.8 reduce-scatter.16

commit v2 on v0

v2 whole, which is shorter than its diff:
```python
import functools

import jax
import jax.numpy as jnp
from jax import lax
from jax.experimental import pallas as pl
from jax.experimental.pallas import tpu as pltpu
from jax.sharding import PartitionSpec as P

MESH = pl.DeviceIdType.MESH
f32, bf16 = jnp.float32, jnp.bfloat16

noise_sigma = 0.5
root_coeff = 0.7978845608028654
cubic_coeff = 0.044715

FEAT, HID, TOK, RANK = 1152, 1152, 512, 64
NX, NZ, NT = 4, 8, 16
SHARD = HID // NX
HALF = SHARD // 2
OWN = FEAT // NT
LANES = TOK // 4
WIDE = TOK + 2 * RANK
MESSAGES = 112


def gelu_pair(value):
    inner = root_coeff * (value + cubic_coeff * value * value * value)
    bend = jnp.tanh(inner)
    result = 0.5 * value * (1.0 + bend)
    slope = 0.5 * (1.0 + bend) + 0.5 * value * (1.0 - bend * bend) * root_coeff * (
        1.0 + 3.0 * cubic_coeff * value * value
    )
    return (result, slope)


def dot(left, right):
    return jnp.dot(left, right, preferred_element_type=f32)


def dot_nt(left, right):
    return lax.dot_general(left, right, (((1,), (1,)), ((), ())), preferred_element_type=f32)


def kernel(
    scale_grad,
    tokcot_in,
    wgu_in,
    wdn_in,
    ngu_in,
    ndn_in,
    left_t,
    right_n,
    down_left_t,
    down_right_n,
    out_ref,
    feature_ref,
    hidden_ref,
    weights,
    noisy,
    noisy_t,
    gathered,
    acts,
    left_c,
    right_c,
    lows,
    ranks,
    part,
    core_in,
    y_out,
    y_in,
    back,
    pieces,
    up_in,
    down_in,
    cross_in,
    draw_in,
    adapters,
    tall,
    hid_part,
    hid_core,
    hid_y_out,
    hid_y_in,
    hid_draw,
    hid_all,
    send_sem,
    recv_sem,
    local_sem,
):
    tensor = lax.axis_index("tensor")
    x = lax.axis_index("draw")
    batch = lax.axis_index("batch")
    yl, z = tensor // NZ, tensor % NZ
    yh, core = batch // 2, batch % 2

    def ring(value, count):
        return (value + count) % count

    x_peers = [{"draw": ring(x + o, NX)} for o in (1, 2, 3)]
    x_right, x_left = x_peers[0], x_peers[2]
    z_up = {"tensor": yl * NZ + ring(z + 1, NZ)}
    z_down = {"tensor": yl * NZ + ring(z - 1, NZ)}
    y_lo = {"tensor": (1 - yl) * NZ + z}
    to_core = {"batch": yh * 2 + 1 - core}
    y_hi = {"batch": (1 - yh) * 2 + core}

    count = [0]
    started = []

    def send(src, dst, where):
        at = count[0]
        count[0] += 1
        assert at < MESSAGES
        copy = pltpu.make_async_remote_copy(
            src_ref=src,
            dst_ref=dst,
            send_sem=send_sem.at[at],
            recv_sem=recv_sem.at[at],
            device_id=where,
            device_id_type=MESH,
        )
        copy.start()
        started.append(copy)
        return copy

    barrier = pltpu.get_barrier_semaphore()
    partners = [*x_peers, z_up, z_down, y_lo, to_core, y_hi]
    for where in partners:
        pl.semaphore_signal(barrier, inc=1, device_id=where, device_id_type=MESH)
    pl.semaphore_wait(barrier, len(partners))

    def rows(owner, first=0, size=SHARD):
        return pl.ds(pl.multiple_of(owner * SHARD + first, 16), size)

    own_copy = pltpu.make_async_copy(tokcot_in, gathered.at[tensor], local_sem.at[0])
    own_copy.start()
    y_copy = send(tokcot_in, gathered.at[tensor], y_lo)
    to_right = [send(wgu_in.at[k], weights.at[k, rows(x)], x_right) for k in (0, 1)]
    to_left = [send(wgu_in.at[k], weights.at[k, rows(x)], x_left) for k in (0, 1)]
    to_right.append(send(wdn_in, weights.at[2, rows(x)], x_right))
    to_left.append(send(wdn_in, weights.at[2, rows(x)], x_left))
    locals_ = [
        pltpu.make_async_copy(ngu_in.at[0], noisy_t.at[0], local_sem.at[1]),
        pltpu.make_async_copy(ngu_in.at[1], noisy_t.at[1], local_sem.at[2]),
        pltpu.make_async_copy(ndn_in, noisy.at[2], local_sem.at[3]),
        pltpu.make_async_copy(wgu_in.at[0], weights.at[0, rows(x)], local_sem.at[4]),
        pltpu.make_async_copy(wgu_in.at[1], weights.at[1, rows(x)], local_sem.at[5]),
        pltpu.make_async_copy(wdn_in, weights.at[2, rows(x)], local_sem.at[6]),
    ]
    for copy in locals_:
        copy.start()

    def gather_rings(ref):
        def hop(step, half, up):
            at = half * NZ + (ring(z - step, NZ) if up else ring(z + step, NZ))
            return send(ref.at[at], ref.at[at], z_up if up else z_down)

        flight = {}
        for half in (0, 1):
            for up in (True, False):
                flight[half, up] = hop(0, half, up)
        for step in (1, 2, 3, 4):
            for half in (0, 1):
                for up in (True, False):
                    last = 4 if (half == 0) == up else 3
                    if step > last:
                        continue
                    flight[half, up].wait_recv()
                    if step < last:
                        flight[half, up] = hop(step, half, up)
            yield step

    def flip(source, target, first, last):
        def body(strip, _):
            k, at = strip // 9, pl.ds(pl.multiple_of((strip % 9) * 128, 128), 128)
            target[k, :, at] = source[k, at, :].T
            return 0

        lax.fori_loop(first, last, body, 0)

    for k in (0, 1):
        left_c[k] = left_t[k].T
        right_c[k] = right_n[k].T
    left_c[2] = down_right_n[...].T
    right_c[2] = down_left_t[...].T
    own_copy.wait()
    y_copy.wait_recv()
    rings = gather_rings(gathered)
    locals_[0].wait()
    locals_[1].wait()
    flip(noisy_t, noisy, 0, 5)
    next(rings)
    flip(noisy_t, noisy, 5, 10)
    next(rings)
    flip(noisy_t, noisy, 10, 15)
    next(rings)
    flip(noisy_t, noisy, 15, 18)
    next(rings)

    def unpack(m, _):
        first, second = gathered[2 * m].astype(f32), gathered[2 * m + 1].astype(f32)
        at = pl.ds(pl.multiple_of(m * 2 * OWN, 16), 2 * OWN)
        acts[0, at, :] = jnp.concatenate([first[:OWN], second[:OWN]]).astype(bf16)
        acts[1, at, :] = jnp.concatenate([first[OWN:], second[OWN:]]).astype(bf16)
        return 0

    lax.fori_loop(0, NZ, unpack, 0)
    lows[0] = dot(left_t[0], acts[0]).astype(bf16)
    lows[1] = dot(left_t[1], acts[0]).astype(bf16)
    lows[2] = dot(down_right_n[...], acts[1]).astype(bf16)
    for copy in locals_[2:]:
        copy.wait()

    x_l, x_r, x_o = ring(x - 1, NX), ring(x + 1, NX), ring(x + 2, NX)
    fwd_right, fwd_left = [], []

    def forward(k):
        to_right[k].wait_recv()
        at = weights.at[k, rows(x_l, 0, HALF)]
        fwd_right.append(send(at, at, x_right))
        to_left[k].wait_recv()
        at = weights.at[k, rows(x_r, HALF, HALF)]
        fwd_left.append(send(at, at, x_left))

    def spread(j, owner):
        def body(k, _):
            at = rows(owner)
            noisy[k, at, :] = (
                weights[k, at, :].astype(f32) * (1.0 + noise_sigma * noisy[k, at, :].astype(f32))
            ).astype(bf16)
            total = dot(noisy[k, at, :], acts[k // 2]) + dot(right_c[k, at, :], lows[k])
            for b in range(4):
                part[j, b % 2, b // 2, k] = total[:, b * LANES : (b + 1) * LANES].astype(bf16)
            return 0

        lax.fori_loop(0, 3, body, 0)
        return send(part.at[j, 1 - core], core_in.at[j], to_core)

    def cores(j, copy):
        copy.wait_recv()
        y_out[j] = (
            part[j, core, 1 - yh].astype(f32) + core_in[j, 1 - yh].astype(f32)
        ).astype(bf16)
        return send(y_out.at[j], y_in.at[j], y_hi)

    def bend(j, owner, copy):
        copy.wait_recv()
        at = rows(owner)

        def whole(k):
            return (
                part[j, core, yh, k].astype(f32)
                + core_in[j, yh, k].astype(f32)
                + y_in[j, k].astype(f32)
            )

        gate, up, grad = whole(0), whole(1), whole(2)
        active, slope = gelu_pair(gate)
        back[batch, 0, at, :] = (grad * up * slope).astype(bf16)
        back[batch, 1, at, :] = (grad * active).astype(bf16)
        back[batch, 2, at, :] = (active * up).astype(bf16)
        mine = back.at[batch, :, at]
        return [send(mine, mine, y_hi), send(mine, mine, to_core)]

    def share(owner, copies):
        copies[0].wait_recv()
        far = back.at[(1 - yh) * 2 + core, :, rows(owner)]
        copies.append(send(far, far, to_core))

    def finish(copies):
        copies[1].wait_recv()
        copies[2].wait_recv()

    forward(0)
    c0 = spread(0, x)
    forward(1)
    c0 = cores(0, c0)
    forward(2)
    c1 = spread(1, x_l)
    c0 = bend(0, x, c0)
    c1 = cores(1, c1)
    c2 = spread(2, x_r)
    share(x, c0)
    c1 = bend(1, x_l, c1)
    c2 = cores(2, c2)
    finish(c0)
    share(x_l, c1)
    c2 = bend(2, x_r, c2)
    finish(c1)
    share(x_r, c2)
    finish(c2)
    for k in range(3):
        fwd_right[k].wait_recv()
        fwd_left[k].wait_recv()
    c3 = spread(3, x_o)
    flip(noisy, noisy_t, 0, 9)
    c3 = cores(3, c3)
    flip(noisy, noisy_t, 9, 18)
    c3 = bend(3, x_o, c3)
    flip(noisy, noisy_t, 18, 27)
    share(x_o, c3)
    finish(c3)

    def all_tokens(k):
        return jnp.concatenate([back[b, k] for b in range(4)], axis=1)

    for k in range(3):
        values = all_tokens(k)
        sheet = right_n[k] if k < 2 else down_left_t[...]
        ranks[pl.ds(k * RANK, RANK), :] = dot(sheet, values).astype(bf16)
        hid_part[pl.ds(k * RANK, RANK), :] = dot_nt(lows[k], values).astype(bf16)

    h1 = send(
        hid_part.at[pl.ds(pl.multiple_of((1 - core) * 96, 16), 96)], hid_core, to_core
    )

    def outputs(m, _):
        at = pl.ds(pl.multiple_of(m * SHARD, 16), SHARD)
        out = dot(noisy_t[2, at, :], all_tokens(2)) + dot(left_c[2, at, :], ranks[128:192, :])
        grad = dot(noisy_t[0, at, :], all_tokens(0)) + dot(left_c[0, at, :], ranks[0:64, :])
        grad = grad + dot(noisy_t[1, at, :], all_tokens(1)) + dot(left_c[1, at, :], ranks[64:128, :])
        right_side = dot_nt(acts[1, at, :], ranks[64:192, :])
        left_side = dot_nt(acts[0, at, :], ranks[0:128, :])
        for i in range(4):
            cut = slice(i * OWN, (i + 1) * OWN)
            pieces[4 * m + i, :, :TOK] = jnp.concatenate([out[cut], grad[cut]]).astype(bf16)
            pieces[4 * m + i, :, TOK:] = jnp.concatenate(
                [right_side[cut], left_side[cut]]
            ).astype(bf16)
        return 0

    lax.fori_loop(0, 4, outputs, 0)

    def pass_on(step, half, up, copy):
        target = half * NZ + (ring(z + 4 - step, NZ) if up else ring(z - 4 + step, NZ))
        box = (up_in if up else down_in).at[step, half]
        if copy is not None:
            copy.wait_recv()
            came = (up_in if up else down_in)[step - 1, half]
            pieces[target] = (pieces[target].astype(f32) + came.astype(f32)).astype(bf16)
        return send(pieces.at[target], box, z_up if up else z_down)

    flight = {}
    flight[0, True] = pass_on(0, 0, True, None)
    flight[1, False] = pass_on(0, 1, False, None)
    flight[1, True] = pass_on(1, 1, True, None)
    flight[0, False] = pass_on(1, 0, False, None)

    h1.wait_recv()
    own_rows = pl.ds(pl.multiple_of(core * 96 + yh * 48, 16), 48)
    far_rows = pl.ds(pl.multiple_of(core * 96 + (1 - yh) * 48, 16), 48)
    own_half = pl.ds(pl.multiple_of(yh * 48, 16), 48)
    far_half = pl.ds(pl.multiple_of((1 - yh) * 48, 16), 48)
    hid_y_out[...] = (
        hid_part[far_rows, :].astype(f32) + hid_core[far_half, :].astype(f32)
    ).astype(bf16)
    h2 = send(hid_y_out, hid_y_in, y_hi)

    flight[0, True] = pass_on(1, 0, True, flight[0, True])
    flight[1, False] = pass_on(1, 1, False, flight[1, False])

    h2.wait_recv()
    hid_draw[x] = (
        hid_part[own_rows, :].astype(f32)
        + hid_core[own_half, :].astype(f32)
        + hid_y_in[...].astype(f32)
    ).astype(bf16)
    h3 = [send(hid_draw.at[x], hid_draw.at[x], where) for where in x_peers]

    flight[1, True] = pass_on(2, 1, True, flight[1, True])
    flight[0, False] = pass_on(2, 0, False, flight[0, False])
    flight[0, True] = pass_on(2, 0, True, flight[0, True])
    flight[1, False] = pass_on(2, 1, False, flight[1, False])

    for copy in h3:
        copy.wait_recv()
    total = (hid_draw[0].astype(f32) + hid_draw[1].astype(f32)) + (
        hid_draw[2].astype(f32) + hid_draw[3].astype(f32)
    )
    hid_all[own_rows, :] = (scale_grad * total).astype(bf16)
    h4 = [
        send(hid_all.at[own_rows], hid_all.at[own_rows], y_hi),
        send(hid_all.at[own_rows], hid_all.at[own_rows], to_core),
    ]

    flight[1, True] = pass_on(3, 1, True, flight[1, True])
    flight[0, False] = pass_on(3, 0, False, flight[0, False])
    flight[0, True] = pass_on(3, 0, True, flight[0, True])
    flight[1, False] = pass_on(3, 1, False, flight[1, False])

    h4[0].wait_recv()
    h4.append(send(hid_all.at[far_rows], hid_all.at[far_rows], to_core))

    for copy in flight.values():
        copy.wait_recv()

    def over_z(half):
        return (
            pieces[half * NZ + z].astype(f32)
            + up_in[3, half].astype(f32)
            + down_in[3, half].astype(f32)
        )

    y_piece = (1 - yl) * NZ + z
    pieces[y_piece] = over_z(1 - yl).astype(bf16)
    cross = send(pieces.at[y_piece], cross_in, y_lo)
    mine = over_z(yl)
    h4[1].wait_recv()
    h4[2].wait_recv()
    hidden_ref[...] = hid_all[...]
    cross.wait_recv()
    mine = mine + cross_in[...].astype(f32)
    draw_in[x] = mine[:, TOK:].astype(bf16)
    d1 = [send(draw_in.at[x], draw_in.at[x], where) for where in x_peers]
    out_ref[...] = mine[:, :TOK].astype(bf16)
    for copy in d1:
        copy.wait_recv()
    total = (draw_in[0].astype(f32) + draw_in[1].astype(f32)) + (
        draw_in[2].astype(f32) + draw_in[3].astype(f32)
    )
    adapters[tensor] = (scale_grad * total).astype(bf16)
    y_copy = send(adapters.at[tensor], adapters.at[tensor], y_lo)
    y_copy.wait_recv()
    for _ in gather_rings(adapters):
        pass
    for t in range(NT):
        both = adapters[t].astype(f32)
        tall[1, t * OWN : (t + 1) * OWN, :] = both[:OWN]
        tall[0, t * OWN : (t + 1) * OWN, :] = both[OWN:]
    feature_ref[: 2 * RANK, :] = tall[0].T.astype(bf16)
    feature_ref[2 * RANK :, :] = tall[1].T[RANK:].astype(bf16)
    for copy in started:
        copy.wait_send()


def on_device(
    tokens,
    cotangent,
    gate_up_weight,
    down_weight,
    gate_up_noise,
    down_noise,
    gate_up_left,
    gate_up_right,
    down_left,
    down_right,
):
    scale_grad = (NX * TOK) ** (-0.5)
    vmem, anywhere = pl.BlockSpec(memory_space=pltpu.VMEM), pl.BlockSpec(memory_space=pl.ANY)
    tokcot = jnp.concatenate([tokens[0].T, cotangent[0].T])
    scratch = [
        pltpu.VMEM((3, HID, FEAT), bf16),
        pltpu.VMEM((3, HID, FEAT), bf16),
        pltpu.VMEM((3, FEAT, HID), bf16),
        pltpu.VMEM((NT, 2 * OWN, TOK), bf16),
        pltpu.VMEM((2, FEAT, TOK), bf16),
        pltpu.VMEM((3, FEAT, RANK), bf16),
        pltpu.VMEM((3, HID, RANK), bf16),
        pltpu.VMEM((3, RANK, TOK), bf16),
        pltpu.VMEM((3 * RANK, TOK), bf16),
        pltpu.VMEM((NX, 2, 2, 3, SHARD, LANES), bf16),
        pltpu.VMEM((NX, 2, 3, SHARD, LANES), bf16),
        pltpu.VMEM((NX, 3, SHARD, LANES), bf16),
        pltpu.VMEM((NX, 3, SHARD, LANES), bf16),
        pltpu.VMEM((4, 3, HID, LANES), bf16),
        pltpu.VMEM((NT, 2 * OWN, WIDE), bf16),
        pltpu.VMEM((4, 2, 2 * OWN, WIDE), bf16),
        pltpu.VMEM((4, 2, 2 * OWN, WIDE), bf16),
        pltpu.VMEM((2 * OWN, WIDE), bf16),
        pltpu.VMEM((NX, 2 * OWN, 2 * RANK), bf16),
        pltpu.VMEM((NT, 2 * OWN, 2 * RANK), bf16),
        pltpu.VMEM((2, FEAT, 2 * RANK), f32),
        pltpu.VMEM((3 * RANK, HID), bf16),
        pltpu.VMEM((96, HID), bf16),
        pltpu.VMEM((48, HID), bf16),
        pltpu.VMEM((48, HID), bf16),
        pltpu.VMEM((NX, 48, HID), bf16),
        pltpu.VMEM((3 * RANK, HID), bf16),
        pltpu.SemaphoreType.DMA((MESSAGES,)),
        pltpu.SemaphoreType.DMA((MESSAGES,)),
        pltpu.SemaphoreType.DMA((8,)),
    ]
    both, feature, hidden = pl.pallas_call(
        functools.partial(kernel, scale_grad),
        out_shape=(
            jax.ShapeDtypeStruct((2 * OWN, TOK), bf16),
            jax.ShapeDtypeStruct((3 * RANK, FEAT), bf16),
            jax.ShapeDtypeStruct((3 * RANK, HID), bf16),
        ),
        in_specs=[anywhere] * 5 + [vmem] * 4,
        out_specs=(vmem, vmem, vmem),
        scratch_shapes=scratch,
        compiler_params=pltpu.CompilerParams(
            collective_id=0, has_side_effects=True, vmem_limit_bytes=60 * 2**20
        ),
    )(
        tokcot,
        jnp.swapaxes(gate_up_weight, 1, 2),
        down_weight,
        gate_up_noise[0],
        down_noise[0],
        jnp.swapaxes(gate_up_left, 1, 2),
        gate_up_right,
        down_left.T,
        down_right,
    )
    return (
        both[:OWN].T[None],
        both[OWN:].T[None],
        jnp.swapaxes(feature[: 2 * RANK].reshape(2, RANK, FEAT), 1, 2),
        hidden[: 2 * RANK].reshape(2, RANK, HID),
        hidden[2 * RANK :].T,
        feature[2 * RANK :],
    )


def solution(mesh):
    in_specs = (
        P("draw", None, ("batch", "tensor")),
        P("draw", None, ("batch", "tensor")),
        P(None, "batch", ("tensor", "draw")),
        P(("tensor", "draw"), "batch"),
        P("draw", None, "batch", "tensor"),
        P("draw", "tensor", "batch"),
        P(None, "batch", None),
        P(None, None, "tensor"),
        P("tensor", None),
        P(None, "batch"),
    )
    out_specs = (
        P("draw", None, ("batch", "tensor")),
        P("draw", None, ("batch", "tensor")),
        P(None, "batch", None),
        P(None, None, "tensor"),
        P("tensor", None),
        P(None, "batch"),
    )
    return jax.shard_map(
        on_device, mesh=mesh, in_specs=in_specs, out_specs=out_specs, check_vma=False
    )
```

time: 1300 us -> 183 us (0.14)
  waiting for transfers between devices: 1200 us -> 0 us
  Pallas kernels: 0 us -> 173 us
  matrix products: 48.3 us -> 0 us
  local copies, waits for them, and re-layouts: 23.2 us -> 8.14 us
  between operations: 14.4 us -> 0.64 us
    psum x2 -> x0, waiting for transfers between devices: 708 us -> none  [the longest x1 587 us: on_device(): lax.psum((left_term, down_right_term), ('tensor', 'draw'))]
    all_gather x6 -> x0, waiting for transfers between devices: 275 us -> none  [the longest x1 68.2 us: on_device(): cot_all = lax.all_gather(cotangent[0], 'tensor', axis=1, tiled=True)]
    reduce_scatter x3 -> x0, waiting for transfers between devices: 202 us -> none  [the longest x1 70.9 us: on_device(): lax.psum_scatter(in_part.astype(jnp.bfloat16), 'tensor', scatter_dimensio...]
    pallas_call x0 -> x1, Pallas kernels: none -> 173 us  [on_device(): pl.pallas_call(functools.partial(kernel, scale_grad), out_shape=(jax.Shap...]
    dot_general x16 -> x0, matrix products: 48.3 us -> none  [the longest x4 8.49 us: highest(): jnp.dot(left, right, precision=lax.Precision.HIGHEST, preferred_element_t...]
    all_gather x1 -> x0, local copies, waits for them, and re-layouts: 16.5 us -> none  [on_device(): lax.all_gather(gate_up_weight, 'draw', axis=2, tiled=True)]
    unnamed x13 -> x0, waiting for transfers between devices: 16.2 us -> none
  transfers between devices with their start and end apart: 12 -> 0, of which waited for: 12 -> 0; matrix products, arithmetic and copies ran while one was open for 6% -> 0% of each run, Pallas kernels for 0% -> 0%
where the time goes in v2:
time: 183 us
  Pallas kernels  173 us (95%)
  local copies, waits for them, and re-layouts  8.14 us (4%)
    pallas_call x1, Pallas kernels, on_device(): pl.pallas_call(functools.partial(kernel, scale_grad), out_shape=(jax.Shap...  173 us

profile of v2, /device:TPU:32, one launch (start us, length us, event | category | flops | bytes accessed | tf_op | source)
XLA Modules:
  0.0 182.9 jit_solution(9983198926516011932)
XLA Ops:
  0.6 1.6 pad_maximum_fusion.tokcot_in
  2.2 172.5 %shard_map.145 = (bf16[144,512]{1,0:T(8,128)(2,1)}, bf16[192,1152]{1,0:T(8,128)(2,1)}, bf16[192,1152]{1,0:T(8,128)(2,1)}) custom-call(bf16[144,512]{1,0:T(8,128)(2,1)} %pad_maximum_fusion.tokcot_in, bf16[2,288,1152]{2,1,0:T(8,128)(2,1)} %bitcast.27, bf16[288,1152]{1,0:T(8,128)(2,1)} %wdn_in.1, bf16[2,1152,1152]{2,1,0:T(8,128)(2,1)} %bitcast.25, ...), custom_call_target="tpu_custom_call" | custom-call | tf_op jit(solution)/shard_map/pallas_call | solution.py:483
  174.8 1.6 slice_bitcast_fusion.1
  176.3 1.6 slice.23
  177.9 1.7 slice.20
  179.6 1.6 slice_bitcast_fusion
  181.2 1.7 slice.21

commit v3 on v2

v3 whole, which is shorter than its diff:
```python
import functools

import jax
import jax.numpy as jnp
from jax import lax
from jax.experimental import pallas as pl
from jax.experimental.pallas import tpu as pltpu
from jax.sharding import PartitionSpec as P

MESH = pl.DeviceIdType.MESH
f32, bf16 = jnp.float32, jnp.bfloat16

noise_sigma = 0.5
root_coeff = 0.7978845608028654
cubic_coeff = 0.044715

FEAT, HID, TOK, RANK = 1152, 1152, 512, 64
NX, NZ, NT = 4, 8, 16
SHARD = HID // NX
HALF = SHARD // 2
OWN = FEAT // NT
PACK = OWN + 40
LANES = TOK // 4
EARLY = 768
MESSAGES = 128


def gelu_pair(value):
    inner = root_coeff * (value + cubic_coeff * value * value * value)
    bend = jnp.tanh(inner)
    result = 0.5 * value * (1.0 + bend)
    slope = 0.5 * (1.0 + bend) + 0.5 * value * (1.0 - bend * bend) * root_coeff * (
        1.0 + 3.0 * cubic_coeff * value * value
    )
    return (result, slope)


def dot(left, right):
    return jnp.dot(left, right, preferred_element_type=f32)


def dot_nt(left, right):
    return lax.dot_general(left, right, (((1,), (1,)), ((), ())), preferred_element_type=f32)


def kernel(
    scale_grad,
    tokens_in,
    cotangent_in,
    wgu_in,
    wdn_in,
    ngu_in,
    ndn_in,
    left_t,
    right_n,
    down_left_t,
    down_right_n,
    out_ref,
    grad_ref,
    left_ref,
    right_ref,
    down_left_ref,
    down_right_ref,
    weights,
    noisy,
    noisy_t,
    gathered,
    acts,
    left_c,
    right_c,
    right_a,
    lows,
    ranks,
    part,
    core_in,
    y_out,
    y_in,
    back,
    early_out,
    early_grad,
    pieces,
    up_in,
    down_in,
    cross_in,
    rank_out,
    rank_in,
    rank_all,
    draw_in,
    adapters,
    tall,
    hid_part,
    hid_core,
    hid_y_out,
    hid_y_in,
    hid_draw,
    hid_all,
    send_sem,
    recv_sem,
    local_sem,
):
    tensor = lax.axis_index("tensor")
    x = lax.axis_index("draw")
    batch = lax.axis_index("batch")
    yl, z = tensor // NZ, tensor % NZ
    yh, core = batch // 2, batch % 2

    def ring(value, count):
        return (value + count) % count

    x_peers = [{"draw": ring(x + o, NX)} for o in (1, 2, 3)]
    x_right, x_left = x_peers[0], x_peers[2]
    z_up = {"tensor": yl * NZ + ring(z + 1, NZ)}
    z_down = {"tensor": yl * NZ + ring(z - 1, NZ)}
    y_lo = {"tensor": (1 - yl) * NZ + z}
    to_core = {"batch": yh * 2 + 1 - core}
    y_hi = {"batch": (1 - yh) * 2 + core}

    count = [0]
    started = []

    def send(src, dst, where):
        at = count[0]
        count[0] += 1
        assert at < MESSAGES
        copy = pltpu.make_async_remote_copy(
            src_ref=src,
            dst_ref=dst,
            send_sem=send_sem.at[at],
            recv_sem=recv_sem.at[at],
            device_id=where,
            device_id_type=MESH,
        )
        copy.start()
        started.append(copy)
        return copy

    gathered[tensor] = jnp.concatenate(
        [tokens_in[...].astype(f32), cotangent_in[...].astype(f32)]
    ).astype(bf16)

    barrier = pltpu.get_barrier_semaphore()
    tensor_peers = [(tensor + o) % NT for o in range(1, NT)]
    partners = [*x_peers, to_core, y_hi, *({"tensor": peer} for peer in tensor_peers)]
    for where in partners:
        pl.semaphore_signal(barrier, inc=1, device_id=where, device_id_type=MESH)
    pl.semaphore_wait(barrier, len(partners))

    def rows(owner, first=0, size=SHARD):
        return pl.ds(pl.multiple_of(owner * SHARD + first, 16), size)

    owners = [x, ring(x - 1, NX), ring(x + 1, NX), ring(x + 2, NX)]

    def place(owner):
        away = ring(owner - x, NX)
        turn = (2 * away + 3 * (away // 2)) % 4
        return pl.ds(pl.multiple_of(turn * SHARD, 16), SHARD)

    def block(j):
        return pl.ds(j * SHARD, SHARD)

    y_copy = send(gathered.at[tensor], gathered.at[tensor], y_lo)
    to_right = [send(wgu_in.at[k], weights.at[k, rows(x)], x_right) for k in (0, 1)]
    to_left = [send(wgu_in.at[k], weights.at[k, rows(x)], x_left) for k in (0, 1)]
    to_right.append(send(wdn_in, weights.at[2, rows(x)], x_right))
    to_left.append(send(wdn_in, weights.at[2, rows(x)], x_left))
    locals_ = [
        pltpu.make_async_copy(ngu_in.at[0], noisy_t.at[0], local_sem.at[1]),
        pltpu.make_async_copy(ngu_in.at[1], noisy_t.at[1], local_sem.at[2]),
        pltpu.make_async_copy(wgu_in.at[0], weights.at[0, rows(x)], local_sem.at[3]),
        pltpu.make_async_copy(wgu_in.at[1], weights.at[1, rows(x)], local_sem.at[4]),
        pltpu.make_async_copy(wdn_in, weights.at[2, rows(x)], local_sem.at[5]),
    ]
    locals_ += [
        pltpu.make_async_copy(
            ndn_in.at[rows(owners[j])], noisy.at[2, block(j)], local_sem.at[6 + j]
        )
        for j in range(NX)
    ]
    for copy in locals_:
        copy.start()

    def gather_rings(ref):
        def hop(step, half, up):
            at = half * NZ + (ring(z - step, NZ) if up else ring(z + step, NZ))
            return send(ref.at[at], ref.at[at], z_up if up else z_down)

        flight = {}
        for half in (0, 1):
            for up in (True, False):
                flight[half, up] = hop(0, half, up)
        for step in (1, 2, 3, 4):
            for half in (0, 1):
                for up in (True, False):
                    last = 4 if (half == 0) == up else 3
                    if step > last:
                        continue
                    flight[half, up].wait_recv()
                    if step < last:
                        flight[half, up] = hop(step, half, up)
            yield step

    def flip_noise(first, last):
        def body(strip, _):
            k, at = strip // 9, pl.ds(pl.multiple_of((strip % 9) * 128, 128), 128)
            turned = noisy_t[k, at, :].T
            for i in range(NX):
                noisy[k, place(i), at] = turned[i * SHARD : (i + 1) * SHARD]
            return 0

        lax.fori_loop(first, last, body, 0)

    def flip_back(first, last):
        def body(strip, _):
            k, at = strip // (last - first), pl.ds(
                pl.multiple_of((first + strip % (last - first)) * 128, 128), 128
            )
            noisy_t[k, :, at] = noisy[k, at, :].T
            return 0

        lax.fori_loop(0, 3 * (last - first), body, 0)

    for k in range(3):
        left_c[k] = (left_t[k] if k < 2 else down_right_n[...]).T
        turned = (right_n[k] if k < 2 else down_left_t[...]).T
        for i in range(NX):
            right_c[k, place(i), :] = turned[i * SHARD : (i + 1) * SHARD]
        right_a[k] = right_c[k].T
    y_copy.wait_recv()
    rings = gather_rings(gathered)
    locals_[0].wait()
    locals_[1].wait()
    flip_noise(0, 5)
    next(rings)
    flip_noise(5, 10)
    next(rings)
    flip_noise(10, 15)
    next(rings)
    flip_noise(15, 18)
    next(rings)

    def unpack(m, _):
        first, second = gathered[2 * m].astype(f32), gathered[2 * m + 1].astype(f32)
        at = pl.ds(pl.multiple_of(m * 2 * OWN, 16), 2 * OWN)
        acts[0, at, :] = jnp.concatenate([first[:OWN], second[:OWN]]).astype(bf16)
        acts[1, at, :] = jnp.concatenate([first[OWN:], second[OWN:]]).astype(bf16)
        return 0

    lax.fori_loop(0, NZ, unpack, 0)
    lows[0] = dot(left_t[0], acts[0]).astype(bf16)
    lows[1] = dot(left_t[1], acts[0]).astype(bf16)
    lows[2] = dot(down_right_n[...], acts[1]).astype(bf16)
    for copy in locals_[2:]:
        copy.wait()

    x_l, x_r = owners[1], owners[2]
    fwd_right, fwd_left = [], []

    def forward(k):
        to_right[k].wait_recv()
        at = weights.at[k, rows(x_l, 0, HALF)]
        fwd_right.append(send(at, at, x_right))
        to_left[k].wait_recv()
        at = weights.at[k, rows(x_r, HALF, HALF)]
        fwd_left.append(send(at, at, x_left))

    def spread(j):
        def body(k, _):
            noisy[k, block(j), :] = (
                weights[k, rows(owners[j]), :].astype(f32)
                * (1.0 + noise_sigma * noisy[k, block(j), :].astype(f32))
            ).astype(bf16)
            total = dot(noisy[k, block(j), :], acts[k // 2])
            total = total + dot(right_c[k, block(j), :], lows[k])
            for b in range(4):
                part[j, b % 2, b // 2, k] = total[:, b * LANES : (b + 1) * LANES].astype(bf16)
            return 0

        lax.fori_loop(0, 3, body, 0)
        return send(part.at[j, 1 - core], core_in.at[j], to_core)

    def cores(j, copy):
        copy.wait_recv()
        y_out[j] = (
            part[j, core, 1 - yh].astype(f32) + core_in[j, 1 - yh].astype(f32)
        ).astype(bf16)
        return send(y_out.at[j], y_in.at[j], y_hi)

    def bend(j, copy):
        copy.wait_recv()
        at = block(j)

        def whole(k):
            return (
                part[j, core, yh, k].astype(f32)
                + core_in[j, yh, k].astype(f32)
                + y_in[j, k].astype(f32)
            )

        gate, up, grad = whole(0), whole(1), whole(2)
        active, slope = gelu_pair(gate)
        back[batch, 0, at, :] = (grad * up * slope).astype(bf16)
        back[batch, 1, at, :] = (grad * active).astype(bf16)
        back[batch, 2, at, :] = (active * up).astype(bf16)
        mine = back.at[batch, :, at]
        return [send(mine, mine, y_hi), send(mine, mine, to_core)]

    def share(j, copies):
        copies[0].wait_recv()
        far = back.at[(1 - yh) * 2 + core, :, block(j)]
        copies.append(send(far, far, to_core))

    def finish(j, copies):
        copies[1].wait_recv()
        copies[2].wait_recv()
        turned = [
            dot_nt(jnp.concatenate([back[b, k, block(j), :] for b in range(4)], axis=1), lows[k])
            for k in range(3)
        ]
        hid_part[rows(owners[j]), :] = jnp.concatenate(turned + turned[2:], axis=1).astype(bf16)

    def all_tokens(k, first=0, last=HID):
        return jnp.concatenate([back[b, k, first:last, :] for b in range(4)], axis=1)

    forward(0)
    c0 = spread(0)
    forward(1)
    c0 = cores(0, c0)
    forward(2)
    c1 = spread(1)
    c2 = spread(2)
    c0 = bend(0, c0)
    c1 = cores(1, c1)
    c2 = cores(2, c2)
    flip_back(0, 6)
    share(0, c0)
    c1 = bend(1, c1)
    c2 = bend(2, c2)
    finish(0, c0)
    for k in range(3):
        fwd_right[k].wait_recv()
        fwd_left[k].wait_recv()
    c3 = spread(3)
    share(1, c1)
    share(2, c2)
    c3 = cores(3, c3)
    finish(1, c1)
    finish(2, c2)

    def early(m, _):
        at = pl.ds(pl.multiple_of(m * SHARD, 16), SHARD)
        early_out[at, :] = dot(noisy_t[2, at, :EARLY], all_tokens(2, 0, EARLY))
        early_grad[at, :] = dot(noisy_t[0, at, :EARLY], all_tokens(0, 0, EARLY)) + dot(
            noisy_t[1, at, :EARLY], all_tokens(1, 0, EARLY)
        )
        return 0

    flip_back(6, 9)
    lax.fori_loop(0, 4, early, 0)
    c3 = bend(3, c3)
    share(3, c3)
    finish(3, c3)

    full = jnp.concatenate([dot(right_a[k], all_tokens(k)) for k in range(3)])
    ranks[...] = full.astype(bf16)
    for unit in range(NT):
        down, across = unit // 4 * 48, unit % 4 * 128
        rank_out[unit] = full[down : down + 48, across : across + 128].astype(bf16)
    r1 = [
        send(rank_out.at[peer], rank_in.at[o], {"tensor": peer})
        for o, peer in enumerate(tensor_peers)
    ]

    h1 = send(
        hid_part.at[pl.ds(pl.multiple_of((1 - core) * 576, 16), 576)], hid_core, to_core
    )

    def outputs(half, group):
        m = half * 2 + group
        at = pl.ds(pl.multiple_of(m * SHARD, 16), SHARD)
        out = early_out[at, :] + dot(noisy_t[2, at, EARLY:], all_tokens(2, EARLY))
        out = out + dot(left_c[2, at, :], ranks[128:192, :])
        grad = early_grad[at, :] + dot(noisy_t[0, at, EARLY:], all_tokens(0, EARLY))
        grad = grad + dot(noisy_t[1, at, EARLY:], all_tokens(1, EARLY))
        grad = grad + dot(left_c[0, at, :], ranks[0:64, :]) + dot(left_c[1, at, :], ranks[64:128, :])
        for i in range(4):
            cut = slice(i * OWN, (i + 1) * OWN)
            pieces[4 * m + i] = jnp.concatenate([out[cut], grad[cut]]).astype(bf16)
        return group

    def pass_on(step, half, up, copy):
        target = half * NZ + (ring(z + 4 - step, NZ) if up else ring(z - 4 + step, NZ))
        box = (up_in if up else down_in).at[step, half]
        if copy is not None:
            copy.wait_recv()
            came = (up_in if up else down_in)[step - 1, half]
            pieces[target] = (pieces[target].astype(f32) + came.astype(f32)).astype(bf16)
        return send(pieces.at[target], box, z_up if up else z_down)

    flight = {}

    def go(step, half, up):
        flight[half, up] = pass_on(step, half, up, flight.get((half, up)))

    lax.fori_loop(0, 2, outputs, 1 - z // 4)
    go(0, 0, True)
    go(0, 1, False)
    for copy in r1:
        copy.wait_recv()
    total = rank_out[tensor].astype(f32)
    for o in range(NT - 1):
        total = total + rank_in[o].astype(f32)
    rank_all[tensor] = total.astype(bf16)
    r2 = [
        send(rank_all.at[tensor], rank_all.at[tensor], {"tensor": peer}) for peer in tensor_peers
    ]
    lax.fori_loop(0, 2, outputs, z // 4)
    go(1, 1, True)
    go(1, 0, False)

    h1.wait_recv()
    own_rows = pl.ds(pl.multiple_of(core * 576 + yh * SHARD, 16), SHARD)
    far_rows = pl.ds(pl.multiple_of(core * 576 + (1 - yh) * SHARD, 16), SHARD)
    own_half = pl.ds(pl.multiple_of(yh * SHARD, 16), SHARD)
    far_half = pl.ds(pl.multiple_of((1 - yh) * SHARD, 16), SHARD)
    hid_y_out[...] = (
        hid_part[far_rows, :].astype(f32) + hid_core[far_half, :].astype(f32)
    ).astype(bf16)
    h2 = send(hid_y_out, hid_y_in, y_hi)

    go(1, 0, True)
    go(1, 1, False)

    for copy in r2:
        copy.wait_recv()
    full = jnp.concatenate(
        [jnp.concatenate([rank_all[4 * r + c] for c in range(4)], axis=1) for r in range(4)]
    )
    both = dot_nt(gathered[tensor], full)
    third = both[OWN:, 2 * RANK :]
    folded = jnp.concatenate([third[40:], jnp.zeros((8, RANK), f32)])
    folded = jnp.concatenate([third[:40], folded], axis=1)
    draw_in[x] = jnp.concatenate([both[:OWN, : 2 * RANK], folded]).astype(bf16)
    d1 = [send(draw_in.at[x], draw_in.at[x], where) for where in x_peers]

    go(2, 1, True)
    go(2, 0, False)

    h2.wait_recv()
    hid_draw[x] = (
        hid_part[own_rows, :].astype(f32)
        + hid_core[own_half, :].astype(f32)
        + hid_y_in[...].astype(f32)
    ).astype(bf16)
    h3 = [send(hid_draw.at[x], hid_draw.at[x], where) for where in x_peers]

    def over_draws(ref):
        total = (ref[0].astype(f32) + ref[1].astype(f32)) + (ref[2].astype(f32) + ref[3].astype(f32))
        return (scale_grad * total).astype(bf16)

    for copy in d1:
        copy.wait_recv()
    adapters[tensor] = over_draws(draw_in)
    mine = adapters.at[tensor]
    a1 = [
        send(mine, mine, {"tensor": yl * NZ + ring(z + o, NZ)}) for o in (1, 7, 2, 6, 3, 5, 4)
    ]
    a2 = [send(mine, mine, y_lo)]

    go(2, 0, True)
    go(2, 1, False)
    go(3, 1, True)
    go(3, 0, False)

    for copy in h3:
        copy.wait_recv()
    hid_all[own_rows, :] = over_draws(hid_draw)
    h4 = [
        send(hid_all.at[own_rows], hid_all.at[own_rows], y_hi),
        send(hid_all.at[own_rows], hid_all.at[own_rows], to_core),
    ]

    go(3, 0, True)
    go(3, 1, False)

    for o, copy in zip((1, 7, 2, 6, 3, 5, 4), a1):
        copy.wait_recv()
        at = adapters.at[yl * NZ + ring(z - o, NZ)]
        a2.append(send(at, at, y_lo))

    h4[0].wait_recv()
    h4.append(send(hid_all.at[far_rows], hid_all.at[far_rows], to_core))

    for copy in flight.values():
        copy.wait_recv()

    def over_z(half):
        return (
            pieces[half * NZ + z].astype(f32)
            + up_in[3, half].astype(f32)
            + down_in[3, half].astype(f32)
        )

    y_piece = (1 - yl) * NZ + z
    pieces[y_piece] = over_z(1 - yl).astype(bf16)
    cross = send(pieces.at[y_piece], cross_in, y_lo)
    mine = over_z(yl)
    h4[1].wait_recv()
    h4[2].wait_recv()
    turned = hid_all[...].astype(f32).T
    right_ref[0] = turned[:RANK].astype(bf16)
    right_ref[1] = turned[RANK : 2 * RANK].astype(bf16)
    down_left_ref[...] = turned[2 * RANK : 3 * RANK].astype(bf16)
    cross.wait_recv()
    mine = mine + cross_in[...].astype(f32)
    out_ref[...] = mine[:OWN].astype(bf16)
    grad_ref[...] = mine[OWN:].astype(bf16)
    for copy in a2:
        copy.wait_recv()
    for t in range(NT):
        both = adapters[t].astype(f32)
        tall[0, t * OWN : (t + 1) * OWN, :] = both[:OWN]
        tall[1, t * OWN : t * OWN + 40, :RANK] = both[OWN:, :RANK]
        tall[1, t * OWN + 40 : (t + 1) * OWN, :RANK] = both[OWN : OWN + 32, RANK:]
    turned = tall[0].T.astype(bf16)
    left_ref[0] = turned[:RANK]
    left_ref[1] = turned[RANK:]
    down_right_ref[...] = tall[1].T[:RANK].astype(bf16)
    for copy in started:
        copy.wait_send()


def hand_over(*refs):
    for source, target in zip(refs[:6], refs[6:]):
        target[...] = source[...]


def on_device(
    tokens,
    cotangent,
    gate_up_weight,
    down_weight,
    gate_up_noise,
    down_noise,
    gate_up_left,
    gate_up_right,
    down_left,
    down_right,
):
    scale_grad = (NX * TOK) ** (-0.5)
    vmem, anywhere = pl.BlockSpec(memory_space=pltpu.VMEM), pl.BlockSpec(memory_space=pl.ANY)
    scratch = [
        pltpu.VMEM((3, HID, FEAT), bf16),
        pltpu.VMEM((3, HID, FEAT), bf16),
        pltpu.VMEM((3, FEAT, HID), bf16),
        pltpu.VMEM((NT, 2 * OWN, TOK), bf16),
        pltpu.VMEM((2, FEAT, TOK), bf16),
        pltpu.VMEM((3, FEAT, RANK), bf16),
        pltpu.VMEM((3, HID, RANK), bf16),
        pltpu.VMEM((3, RANK, HID), bf16),
        pltpu.VMEM((3, RANK, TOK), bf16),
        pltpu.VMEM((3 * RANK, TOK), bf16),
        pltpu.VMEM((NX, 2, 2, 3, SHARD, LANES), bf16),
        pltpu.VMEM((NX, 2, 3, SHARD, LANES), bf16),
        pltpu.VMEM((NX, 3, SHARD, LANES), bf16),
        pltpu.VMEM((NX, 3, SHARD, LANES), bf16),
        pltpu.VMEM((4, 3, HID, LANES), bf16),
        pltpu.VMEM((FEAT, TOK), f32),
        pltpu.VMEM((FEAT, TOK), f32),
        pltpu.VMEM((NT, 2 * OWN, TOK), bf16),
        pltpu.VMEM((4, 2, 2 * OWN, TOK), bf16),
        pltpu.VMEM((4, 2, 2 * OWN, TOK), bf16),
        pltpu.VMEM((2 * OWN, TOK), bf16),
        pltpu.VMEM((NT, 48, 128), bf16),
        pltpu.VMEM((NT, 48, 128), bf16),
        pltpu.VMEM((NT, 48, 128), bf16),
        pltpu.VMEM((NX, PACK, 2 * RANK), bf16),
        pltpu.VMEM((NT, PACK, 2 * RANK), bf16),
        pltpu.VMEM((2, FEAT, 2 * RANK), f32),
        pltpu.VMEM((HID, 4 * RANK), bf16),
        pltpu.VMEM((HID // 2, 4 * RANK), bf16),
        pltpu.VMEM((SHARD, 4 * RANK), bf16),
        pltpu.VMEM((SHARD, 4 * RANK), bf16),
        pltpu.VMEM((NX, SHARD, 4 * RANK), bf16),
        pltpu.VMEM((HID, 4 * RANK), bf16),
        pltpu.SemaphoreType.DMA((MESSAGES,)),
        pltpu.SemaphoreType.DMA((MESSAGES,)),
        pltpu.SemaphoreType.DMA((10,)),
    ]
    shapes = [
        (OWN, TOK),
        (OWN, TOK),
        (2, RANK, FEAT),
        (2, RANK, HID),
        (RANK, HID),
        (RANK, FEAT),
    ]
    shapes = tuple(jax.ShapeDtypeStruct(shape, bf16) for shape in shapes)
    results = pl.pallas_call(
        functools.partial(kernel, scale_grad),
        out_shape=shapes,
        in_specs=[vmem] * 2 + [anywhere] * 4 + [vmem] * 4,
        out_specs=(vmem,) * 6,
        scratch_shapes=scratch,
        compiler_params=pltpu.CompilerParams(
            collective_id=0, has_side_effects=True, vmem_limit_bytes=62 * 2**20
        ),
    )(
        tokens[0].T,
        cotangent[0].T,
        jnp.swapaxes(gate_up_weight, 1, 2),
        down_weight,
        gate_up_noise[0],
        down_noise[0],
        jnp.swapaxes(gate_up_left, 1, 2),
        gate_up_right,
        down_left.T,
        down_right,
    )
    out, grad, left, right, down_left_grad, down_right_grad = pl.pallas_call(
        hand_over, out_shape=shapes, in_specs=[vmem] * 6, out_specs=(vmem,) * 6
    )(*results)
    return (
        out.T[None],
        grad.T[None],
        jnp.swapaxes(left, 1, 2),
        right,
        down_left_grad.T,
        down_right_grad,
    )


def solution(mesh):
    in_specs = (
        P("draw", None, ("batch", "tensor")),
        P("draw", None, ("batch", "tensor")),
        P(None, "batch", ("tensor", "draw")),
        P(("tensor", "draw"), "batch"),
        P("draw", None, "batch", "tensor"),
        P("draw", "tensor", "batch"),
        P(None, "batch", None),
        P(None, None, "tensor"),
        P("tensor", None),
        P(None, "batch"),
    )
    out_specs = (
        P("draw", None, ("batch", "tensor")),
        P("draw", None, ("batch", "tensor")),
        P(None, "batch", None),
        P(None, None, "tensor"),
        P("tensor", None),
        P(None, "batch"),
    )
    return jax.shard_map(
        on_device, mesh=mesh, in_specs=in_specs, out_specs=out_specs, check_vma=False
    )
```

time: 183 us -> 151 us (0.83)
  Pallas kernels: 173 us -> 149 us
  local copies, waits for them, and re-layouts: 8.14 us -> 0 us
    pallas_call x1 -> x2, Pallas kernels: 173 us -> 149 us  [the longest x1 147 us: on_device(): pl.pallas_call(functools.partial(kernel, scale_grad), out_shape=shapes, i...]
    slice x3 -> x0, local copies, waits for them, and re-layouts: 4.97 us -> none  [the longest x1 1.7 us: on_device(): feature[:2 * RANK].reshape(2, RANK, FEAT)]
where the time goes in v3:
time: 151 us; the launch traced here: 150 us
  Pallas kernels  149 us (99%)
    pallas_call x1, Pallas kernels, on_device(): pl.pallas_call(functools.partial(kernel, scale_grad), out_shape=shapes, i...  147 us

profile of v3, /device:TPU:32, one launch (start us, length us, event | category | flops | bytes accessed | tf_op | source)
XLA Modules:
  0.0 149.6 jit_solution(606289873451609104)
XLA Ops:
  0.6 146.8 %shard_map.145 = (bf16[72,512]{1,0:T(8,128)(2,1)}, bf16[72,512]{1,0:T(8,128)(2,1)}, bf16[2,64,1152]{2,1,0:T(8,128)(2,1)}, bf16[2,64,1152]{2,1,0:T(8,128)(2,1)}, ...) custom-call(bf16[72,512]{1,0:T(8,128)(2,1)} %bitcast.24, bf16[72,512]{1,0:T(8,128)(2,1)} %bitcast.25, ...), custom_call_target="tpu_custom_call" | custom-call | tf_op jit(solution)/shard_map/pallas_call | solution.py:598
  147.5 2.2 %shard_map.146 = (bf16[72,512]{1,0:T(8,128)(2,1)}, bf16[72,512]{1,0:T(8,128)(2,1)}, bf16[2,64,1152]{2,1,0:T(8,128)(2,1)}, bf16[2,64,1152]{2,1,0:T(8,128)(2,1)}, ...) custom-call(bf16[72,512]{1,0:T(8,128)(2,1)} %get-tuple-element.18.refs_0_, bf16[72,512]{1,0:T(8,128)(2,1)} %get-tuple-element.19.refs_1_, ...), custom_call_target="tpu_custom_call" | custom-call | tf_op jit(solution)/shard_map/pallas_call | solution.py:619

commit v4 on v3

v4 whole, which is shorter than its diff:
```python
import functools

import jax
import jax.numpy as jnp
from jax import lax
from jax.experimental import pallas as pl
from jax.experimental.pallas import tpu as pltpu
from jax.sharding import PartitionSpec as P

MESH = pl.DeviceIdType.MESH
f32, bf16 = jnp.float32, jnp.bfloat16

noise_sigma = 0.5
root_coeff = 0.7978845608028654
cubic_coeff = 0.044715

FEAT, HID, TOK, RANK = 1152, 1152, 512, 64
NX, NZ, NT = 4, 8, 16
SHARD = HID // NX
HALF = SHARD // 2
OWN = FEAT // NT
PACK = OWN + 40
LANES = TOK // 4
PARTS = ((0, 80), (80, 64), (144, 80), (224, 64))
PLACES = ((0, 80, 144, 224), (720, 800, 432, 512), (864, 1024, 944, 1088), (288, 368, 576, 656))
BLOCKS = (
    (0, 288, ((0, 0, 288),)),
    (288, 288, ((3, 0, 144), (1, 144, 144))),
    (576, 288, ((3, 144, 144), (1, 0, 144))),
    (864, 160, ((2, 0, 80), (2, 144, 80))),
    (1024, 128, ((2, 80, 64), (2, 224, 64))),
)
HALFT = TOK // 2
EARLY = 768
MESSAGES = 180


def gelu_pair(value):
    inner = root_coeff * (value + cubic_coeff * value * value * value)
    bend = jnp.tanh(inner)
    result = 0.5 * value * (1.0 + bend)
    slope = 0.5 * (1.0 + bend) + 0.5 * value * (1.0 - bend * bend) * root_coeff * (
        1.0 + 3.0 * cubic_coeff * value * value
    )
    return (result, slope)


def dot(left, right):
    return jnp.dot(left, right, preferred_element_type=f32)


def dot_nt(left, right):
    return lax.dot_general(left, right, (((1,), (1,)), ((), ())), preferred_element_type=f32)


def kernel(
    scale_grad,
    tokens_in,
    cotangent_in,
    wgu_in,
    wdn_in,
    ngu_in,
    ndn_in,
    left_t,
    right_n,
    down_left_t,
    down_right_n,
    out_ref,
    grad_ref,
    left_ref,
    right_ref,
    down_left_ref,
    down_right_ref,
    weights,
    noisy,
    noisy_t,
    own_acts,
    gathered,
    gathered_c,
    acts,
    left_c,
    right_c,
    right_a,
    lows,
    ranks,
    part,
    core_in,
    y_out,
    y_in,
    back,
    early_out,
    early_grad,
    pieces,
    up_in,
    down_in,
    cross_in,
    y_pieces,
    y_pieces_in,
    y_up_in,
    y_down_in,
    rank_out,
    rank_in,
    rank_all,
    draw_in,
    adapters,
    tall,
    hid_part,
    hid_core,
    hid_y_out,
    hid_y_in,
    hid_draw,
    hid_all,
    send_sem,
    recv_sem,
    local_sem,
):
    tensor = lax.axis_index("tensor")
    x = lax.axis_index("draw")
    batch = lax.axis_index("batch")
    yl, z = tensor // NZ, tensor % NZ
    yh, core = batch // 2, batch % 2

    def ring(value, count):
        return (value + count) % count

    x_peers = [{"draw": ring(x + o, NX)} for o in (1, 2, 3)]
    x_right, x_left = x_peers[0], x_peers[2]
    z_up = {"tensor": yl * NZ + ring(z + 1, NZ)}
    z_down = {"tensor": yl * NZ + ring(z - 1, NZ)}
    y_lo = {"tensor": (1 - yl) * NZ + z}
    to_core = {"batch": yh * 2 + 1 - core}
    y_hi = {"batch": (1 - yh) * 2 + core}

    count = [0]
    started = []

    def send(src, dst, where):
        at = count[0]
        count[0] += 1
        assert at < MESSAGES
        copy = pltpu.make_async_remote_copy(
            src_ref=src,
            dst_ref=dst,
            send_sem=send_sem.at[at],
            recv_sem=recv_sem.at[at],
            device_id=where,
            device_id_type=MESH,
        )
        copy.start()
        started.append(copy)
        return copy

    def side_by_side(value):
        return jnp.concatenate([value[:, :HALFT], value[:, HALFT:]])

    own_tokens, own_cotangent = tokens_in[...].astype(f32), cotangent_in[...].astype(f32)
    own_acts[...] = jnp.concatenate([own_tokens, own_cotangent]).astype(bf16)
    gathered[tensor] = side_by_side(own_tokens).astype(bf16)
    gathered_c[tensor] = side_by_side(own_cotangent).astype(bf16)

    barrier = pltpu.get_barrier_semaphore()
    tensor_peers = [(tensor + o) % NT for o in range(1, NT)]
    partners = [*x_peers, to_core, y_hi, *({"tensor": peer} for peer in tensor_peers)]
    for where in partners:
        pl.semaphore_signal(barrier, inc=1, device_id=where, device_id_type=MESH)
    pl.semaphore_wait(barrier, len(partners))

    def rows(owner, first=0, size=SHARD):
        return pl.ds(pl.multiple_of(owner * SHARD + first, 16), size)

    owners = [x, ring(x + 1, NX), ring(x + 2, NX), ring(x - 1, NX)]

    def place(owner, piece):
        away = ring(owner - x, NX)
        odd, high = away % 2, away // 2
        right, opposite, left = odd * (1 - high), (1 - odd) * high, odd * high
        first = PLACES[0][piece] * (1 - right - opposite - left) + PLACES[1][piece] * right
        first = first + PLACES[2][piece] * opposite + PLACES[3][piece] * left
        return pl.ds(pl.multiple_of(first, 16), PARTS[piece][1])

    def block(j):
        return pl.ds(BLOCKS[j][0], BLOCKS[j][1])

    y_copy = send(gathered.at[tensor], gathered.at[tensor], y_lo)
    y_copy_c = send(gathered_c.at[tensor], gathered_c.at[tensor], y_lo)
    to_right, to_left = [], []

    def own_shard(half, k):
        source = wgu_in.at[k] if k < 2 else wdn_in
        for flight, turn, where in ((to_right, half, x_right), (to_left, 1 - half, x_left)):
            first = turn * HALF
            flight.append(
                send(source.at[pl.ds(first, HALF)], weights.at[k, rows(x, first, HALF)], where)
            )

    for half in (0, 1):
        for k in (0, 1):
            own_shard(half, k)
    locals_ = [
        pltpu.make_async_copy(ngu_in.at[0], noisy_t.at[0], local_sem.at[1]),
        pltpu.make_async_copy(ngu_in.at[1], noisy_t.at[1], local_sem.at[2]),
        pltpu.make_async_copy(wgu_in.at[0], weights.at[0, rows(x)], local_sem.at[3]),
        pltpu.make_async_copy(wgu_in.at[1], weights.at[1, rows(x)], local_sem.at[4]),
        pltpu.make_async_copy(wdn_in, weights.at[2, rows(x)], local_sem.at[5]),
    ]
    spans = []
    for start, _, parts in BLOCKS:
        for shard, first, size in parts:
            spans.append((start, shard, first, size))
            start += size
    locals_ += [
        pltpu.make_async_copy(
            ndn_in.at[rows(owners[shard], first, size)],
            noisy.at[2, pl.ds(start, size)],
            local_sem.at[6 + at],
        )
        for at, (start, shard, first, size) in enumerate(spans)
    ]
    for copy in locals_:
        copy.start()

    def gather_rings(ref):
        def hop(step, half, up):
            at = half * NZ + (ring(z - step, NZ) if up else ring(z + step, NZ))
            return send(ref.at[at], ref.at[at], z_up if up else z_down)

        flight = {}
        for half in (0, 1):
            for up in (True, False):
                flight[half, up] = hop(0, half, up)
        yield 0
        for step in (1, 2, 3, 4):
            for half in (0, 1):
                for up in (True, False):
                    last = 4 if (half == 0) == up else 3
                    if step > last:
                        continue
                    flight[half, up].wait_recv()
                    if step < last:
                        flight[half, up] = hop(step, half, up)
            yield step

    def flip_noise(first, last):
        def body(strip, _):
            k, at = strip // 9, pl.ds(pl.multiple_of((strip % 9) * 128, 128), 128)
            turned = noisy_t[k, at, :].T
            for i in range(NX):
                for piece, (first, size) in enumerate(PARTS):
                    first += i * SHARD
                    noisy[k, place(i, piece), at] = turned[first : first + size]
            return 0

        lax.fori_loop(first, last, body, 0)

    def flip_back(k_first, k_last, first, last):
        many = last - first

        def body(strip, _):
            k = k_first + strip // many
            at = pl.ds(pl.multiple_of((first + strip % many) * 128, 128), 128)
            noisy_t[k, :, at] = noisy[k, at, :].T
            return 0

        lax.fori_loop(0, (k_last - k_first) * many, body, 0)

    for k in range(3):
        left_c[k] = (left_t[k] if k < 2 else down_right_n[...]).T
        turned = (right_n[k] if k < 2 else down_left_t[...]).T
        for i in range(NX):
            for piece, (first, size) in enumerate(PARTS):
                first += i * SHARD
                right_c[k, place(i, piece), :] = turned[first : first + size]
        right_a[k] = right_c[k].T
    y_copy.wait_recv()
    rings = gather_rings(gathered)
    next(rings)
    locals_[0].wait()
    locals_[1].wait()
    flip_noise(0, 9)
    next(rings)
    flip_noise(9, 18)
    next(rings)
    next(rings)
    next(rings)
    y_copy_c.wait_recv()
    rings = gather_rings(gathered_c)
    next(rings)

    def unpack(source, target):
        def body(m, _):
            one, two = source[2 * m].astype(f32), source[2 * m + 1].astype(f32)
            at = pl.ds(pl.multiple_of(m * 2 * OWN, 16), 2 * OWN)
            acts[target, at, :HALFT] = jnp.concatenate([one[:OWN], two[:OWN]]).astype(bf16)
            acts[target, at, HALFT:] = jnp.concatenate([one[OWN:], two[OWN:]]).astype(bf16)
            return 0

        lax.fori_loop(0, NZ, body, 0)

    x_l, x_r = owners[3], owners[1]
    last = []

    def forward(k, first, size):
        at = weights.at[k, rows(x_l, first, size)]
        last.append(send(at, at, x_right))
        at = weights.at[k, rows(x_r, first + HALF, size)]
        last.append(send(at, at, x_left))

    def spread(j, k_first, k_last):
        start, size, parts = BLOCKS[j]

        def body(k, _):
            at = start
            for shard, first, count in parts:
                here = pl.ds(at, count)
                noisy[k, here, :] = (
                    weights[k, rows(owners[shard], first, count), :].astype(f32)
                    * (1.0 + noise_sigma * noisy[k, here, :].astype(f32))
                ).astype(bf16)
                at += count
            total = dot(noisy[k, block(j), :], acts[k // 2])
            total = total + dot(right_c[k, block(j), :], lows[k])
            for b in range(4):
                part[b % 2, b // 2, k, block(j), :] = total[:, b * LANES : (b + 1) * LANES].astype(
                    bf16
                )
            return 0

        lax.fori_loop(k_first, k_last, body, 0)
        ks = pl.ds(k_first, k_last - k_first)
        return send(part.at[1 - core, :, ks, block(j)], core_in.at[:, ks, block(j)], to_core)

    def cores(j, k_first, k_last, copy):
        copy.wait_recv()
        at, ks = block(j), pl.ds(k_first, k_last - k_first)
        for half in (0, 1):
            for k in range(k_first, k_last):
                y_out[half, k, at, :] = (
                    part[core, half, k, at, :].astype(f32) + core_in[half, k, at, :].astype(f32)
                ).astype(bf16)
        return send(y_out.at[:, ks, at], y_in.at[:, ks, at], y_hi)

    def whole(half, k, at):
        return y_out[half, k, at, :].astype(f32) + y_in[half, k, at, :].astype(f32)

    def bend(j, copy):
        copy.wait_recv()
        at = block(j)
        for half in (0, 1):
            active, _ = gelu_pair(whole(half, 0, at))
            back[core, half, 2, at, :] = (active * whole(half, 1, at)).astype(bf16)
        mine = back.at[core, :, 2, at]
        return send(mine, mine, to_core)

    def bend_grad(j, copy):
        copy.wait_recv()
        at = block(j)
        for half in (0, 1):
            active, slope = gelu_pair(whole(half, 0, at))
            grad = whole(half, 2, at)
            back[core, half, 0, at, :] = (grad * whole(half, 1, at) * slope).astype(bf16)
            back[core, half, 1, at, :] = (grad * active).astype(bf16)
        mine = back.at[core, :, pl.ds(0, 2), at]
        return send(mine, mine, to_core)

    def all_tokens(k, first=0, last=HID):
        return jnp.concatenate([back[b % 2, b // 2, k, first:last, :] for b in range(4)], axis=1)

    def hid_rows(j, ks, lanes):
        start, size, parts = BLOCKS[j]
        turned = [dot_nt(all_tokens(k, start, start + size), lows[k]) for k in ks]
        turned = jnp.concatenate(turned, axis=1).astype(bf16)
        at = 0
        for shard, first, count in parts:
            hid_part[rows(owners[shard], first, count), lanes] = turned[at : at + count]
            at += count

    def finish(j, copy):
        copy.wait_recv()
        hid_rows(j, (2, 2), slice(2 * RANK, 4 * RANK))

    def finish_grad(j, copy):
        copy.wait_recv()
        hid_rows(j, (0, 1), slice(0, 2 * RANK))

    def early_outputs(m, _):
        at = pl.ds(pl.multiple_of(m * SHARD, 16), SHARD)
        early_out[at, :] = dot(noisy_t[2, at, :EARLY], all_tokens(2, 0, EARLY))
        return 0

    def early_grads(m, _):
        at = pl.ds(pl.multiple_of(m * SHARD, 16), SHARD)
        early_grad[at, :] = dot(noisy_t[0, at, :EARLY], all_tokens(0, 0, EARLY)) + dot(
            noisy_t[1, at, :EARLY], all_tokens(1, 0, EARLY)
        )
        return 0

    for k in (0, 1):
        to_right[k].wait_recv()
        to_left[k].wait_recv()
    for k in (0, 1):
        forward(k, 0, 80)
    for k in (0, 1):
        forward(k, 80, 64)
    own_shard(0, 2)
    own_shard(1, 2)
    unpack(gathered, 0)
    lows[0] = dot(left_t[0], acts[0]).astype(bf16)
    lows[1] = dot(left_t[1], acts[0]).astype(bf16)
    for copy in locals_[2:]:
        copy.wait()
    g0 = spread(0, 0, 2)
    g1 = spread(1, 0, 2)
    next(rings)
    g0 = cores(0, 0, 2, g0)
    g1 = cores(1, 0, 2, g1)
    next(rings)
    for k in (2, 3):
        to_right[k].wait_recv()
        to_left[k].wait_recv()
    g2 = spread(2, 0, 2)
    next(rings)
    g2 = cores(2, 0, 2, g2)
    next(rings)
    unpack(gathered_c, 1)
    lows[2] = dot(down_right_n[...], acts[1]).astype(bf16)
    d0 = spread(0, 2, 3)
    g0 = bend(0, g0)
    d0 = cores(0, 2, 3, d0)
    for copy in last[:4]:
        copy.wait_recv()
    g3 = spread(3, 0, 2)
    flip_back(0, 2, 0, 6)
    g3 = cores(3, 0, 2, g3)
    g1 = bend(1, g1)
    finish(0, g0)
    for copy in last[4:8]:
        copy.wait_recv()
    g4 = spread(4, 0, 2)
    finish(1, g1)
    g4 = cores(4, 0, 2, g4)
    flip_back(0, 2, 6, 9)
    g2 = bend(2, g2)
    to_right[4].wait_recv()
    to_left[4].wait_recv()
    forward(2, 0, 80)
    forward(2, 80, 64)
    d1 = spread(1, 2, 3)
    d0 = bend_grad(0, d0)
    finish(2, g2)
    d1 = cores(1, 2, 3, d1)
    g3 = bend(3, g3)
    finish_grad(0, d0)
    finish(3, g3)
    to_right[5].wait_recv()
    to_left[5].wait_recv()
    d2 = spread(2, 2, 3)
    g4 = bend(4, g4)
    d2 = cores(2, 2, 3, d2)
    flip_back(2, 3, 0, 6)
    lax.fori_loop(0, 4, early_outputs, 0)
    finish(4, g4)
    for copy in last[8:10]:
        copy.wait_recv()
    d3 = spread(3, 2, 3)
    d1 = bend_grad(1, d1)
    ranks[pl.ds(2 * RANK, RANK), :] = dot(right_a[2], all_tokens(2)).astype(bf16)
    d3 = cores(3, 2, 3, d3)
    for copy in last[10:]:
        copy.wait_recv()
    d4 = spread(4, 2, 3)
    flip_back(2, 3, 6, 9)
    d4 = cores(4, 2, 3, d4)

    def outputs(half, group):
        m = half * 2 + group
        at = pl.ds(pl.multiple_of(m * SHARD, 16), SHARD)
        out = early_out[at, :] + dot(noisy_t[2, at, EARLY:], all_tokens(2, EARLY))
        out = out + dot(left_c[2, at, :], ranks[128:192, :])
        for i in range(4):
            pieces[4 * m + i] = side_by_side(out[i * OWN : (i + 1) * OWN]).astype(bf16)
        return group

    def pass_on(step, half, up, copy):
        target = half * NZ + (ring(z + 4 - step, NZ) if up else ring(z - 4 + step, NZ))
        box = (up_in if up else down_in).at[step, half]
        if copy is not None:
            copy.wait_recv()
            came = (up_in if up else down_in)[step - 1, half]
            pieces[target] = (pieces[target].astype(f32) + came.astype(f32)).astype(bf16)
        return send(pieces.at[target], box, z_up if up else z_down)

    flight = {}

    def go(step, half, up):
        flight[half, up] = pass_on(step, half, up, flight.get((half, up)))

    lax.fori_loop(0, 2, outputs, 1 - z // 4)
    go(0, 0, True)
    go(0, 1, False)
    lax.fori_loop(0, 2, outputs, z // 4)
    go(1, 1, True)
    go(1, 0, False)
    d2 = bend_grad(2, d2)
    finish_grad(1, d1)
    finish_grad(2, d2)
    d3 = bend_grad(3, d3)
    go(1, 0, True)
    go(1, 1, False)
    lax.fori_loop(0, 4, early_grads, 0)
    d4 = bend_grad(4, d4)
    finish_grad(3, d3)
    finish_grad(4, d4)

    full = jnp.concatenate([dot(right_a[k], all_tokens(k)) for k in (0, 1)]).astype(bf16)
    ranks[: 2 * RANK, :] = full
    full = jnp.concatenate([full, ranks[2 * RANK :, :]])
    for unit in range(NT):
        down, across = unit // 4 * 48, unit % 4 * 128
        rank_out[unit] = full[down : down + 48, across : across + 128]
    r1 = [
        send(rank_out.at[peer], rank_in.at[o], {"tensor": peer})
        for o, peer in enumerate(tensor_peers)
    ]

    h1 = send(
        hid_part.at[pl.ds(pl.multiple_of((1 - core) * 576, 16), 576)], hid_core, to_core
    )

    def grads(half, group):
        m = half * 2 + group
        at = pl.ds(pl.multiple_of(m * SHARD, 16), SHARD)
        grad = early_grad[at, :] + dot(noisy_t[0, at, EARLY:], all_tokens(0, EARLY))
        grad = grad + dot(noisy_t[1, at, EARLY:], all_tokens(1, EARLY))
        grad = grad + dot(left_c[0, at, :], ranks[0:64, :]) + dot(left_c[1, at, :], ranks[64:128, :])
        for i in range(4):
            y_pieces[4 * m + i] = side_by_side(grad[i * OWN : (i + 1) * OWN]).astype(bf16)
        return group

    def cross_y(target):
        at = (1 - yl) * NZ + ring(target, NZ)
        return send(y_pieces.at[at], y_pieces_in.at[ring(target, NZ)], y_lo)

    def y_pass(step, up, copy, arrived):
        target = ring(z + 4 - step, NZ) if up else ring(z - 3 + step, NZ)
        box = y_up_in if up else y_down_in
        arrived.wait_recv()
        total = y_pieces[yl * NZ + target].astype(f32) + y_pieces_in[target].astype(f32)
        if copy is not None:
            copy.wait_recv()
            total = total + box[step - 1].astype(f32)
        y_pieces[yl * NZ + target] = total.astype(bf16)
        return send(y_pieces.at[yl * NZ + target], box.at[step], z_up if up else z_down)

    lax.fori_loop(0, 2, grads, 1 - z // 4)
    crossed = {4: cross_y(z + 4)}
    go(2, 1, True)
    go(2, 0, False)
    lax.fori_loop(0, 2, grads, z // 4)
    for away in (3, -3, 2, -2, 1, -1, 0):
        crossed[away] = cross_y(z + away)
    go(2, 0, True)
    go(2, 1, False)
    for copy in r1:
        copy.wait_recv()
    total = rank_out[tensor].astype(f32)
    for o in range(NT - 1):
        total = total + rank_in[o].astype(f32)
    rank_all[tensor] = total.astype(bf16)
    r2 = [
        send(rank_all.at[tensor], rank_all.at[tensor], {"tensor": peer}) for peer in tensor_peers
    ]
    y_up = y_pass(0, True, None, crossed[4])
    go(3, 1, True)
    go(3, 0, False)

    h1.wait_recv()
    own_rows = pl.ds(pl.multiple_of(core * 576 + yh * SHARD, 16), SHARD)
    far_rows = pl.ds(pl.multiple_of(core * 576 + (1 - yh) * SHARD, 16), SHARD)
    own_half = pl.ds(pl.multiple_of(yh * SHARD, 16), SHARD)
    far_half = pl.ds(pl.multiple_of((1 - yh) * SHARD, 16), SHARD)
    hid_y_out[...] = (
        hid_part[far_rows, :].astype(f32) + hid_core[far_half, :].astype(f32)
    ).astype(bf16)
    h2 = send(hid_y_out, hid_y_in, y_hi)

    y_down = y_pass(0, False, None, crossed[-3])
    go(3, 0, True)
    go(3, 1, False)
    y_up = y_pass(1, True, y_up, crossed[3])

    for copy in r2:
        copy.wait_recv()
    full = jnp.concatenate(
        [jnp.concatenate([rank_all[4 * r + c] for c in range(4)], axis=1) for r in range(4)]
    )
    both = dot_nt(own_acts[...], full)
    third = both[OWN:, 2 * RANK :]
    folded = jnp.concatenate([third[40:], jnp.zeros((8, RANK), f32)])
    folded = jnp.concatenate([third[:40], folded], axis=1)
    draw_in[x] = jnp.concatenate([both[:OWN, : 2 * RANK], folded]).astype(bf16)
    d1 = [send(draw_in.at[x], draw_in.at[x], where) for where in x_peers]

    for copy in flight.values():
        copy.wait_recv()

    def over_z(half):
        return (
            pieces[half * NZ + z].astype(f32)
            + up_in[3, half].astype(f32)
            + down_in[3, half].astype(f32)
        )

    y_piece = (1 - yl) * NZ + z
    pieces[y_piece] = over_z(1 - yl).astype(bf16)
    cross = send(pieces.at[y_piece], cross_in, y_lo)
    y_down = y_pass(1, False, y_down, crossed[-2])
    y_up = y_pass(2, True, y_up, crossed[2])

    def over_draws(ref):
        total = (ref[0].astype(f32) + ref[1].astype(f32)) + (ref[2].astype(f32) + ref[3].astype(f32))
        return (scale_grad * total).astype(bf16)

    for copy in d1:
        copy.wait_recv()
    adapters[tensor] = over_draws(draw_in)
    mine = adapters.at[tensor]
    a1 = [
        send(mine, mine, {"tensor": yl * NZ + ring(z + o, NZ)}) for o in (1, 7, 2, 6, 3, 5, 4)
    ]
    a2 = [send(mine, mine, y_lo)]

    y_down = y_pass(2, False, y_down, crossed[-1])
    y_up = y_pass(3, True, y_up, crossed[1])

    h2.wait_recv()
    hid_draw[x] = (
        hid_part[own_rows, :].astype(f32)
        + hid_core[own_half, :].astype(f32)
        + hid_y_in[...].astype(f32)
    ).astype(bf16)
    h3 = [send(hid_draw.at[x], hid_draw.at[x], where) for where in x_peers]

    cross.wait_recv()
    first = over_z(yl) + cross_in[...].astype(f32)
    out_ref[:, :HALFT] = first[:OWN].astype(bf16)
    out_ref[:, HALFT:] = first[OWN:].astype(bf16)
    for o, copy in zip((1, 7, 2, 6, 3, 5, 4), a1):
        copy.wait_recv()
        at = adapters.at[yl * NZ + ring(z - o, NZ)]
        a2.append(send(at, at, y_lo))

    for copy in h3:
        copy.wait_recv()
    hid_all[own_rows, :] = over_draws(hid_draw)
    h4 = [
        send(hid_all.at[own_rows], hid_all.at[own_rows], y_hi),
        send(hid_all.at[own_rows], hid_all.at[own_rows], to_core),
    ]
    y_up.wait_recv()
    y_down.wait_recv()
    crossed[0].wait_recv()
    second = (
        (y_pieces[yl * NZ + z].astype(f32) + y_pieces_in[z].astype(f32))
        + y_up_in[3].astype(f32)
        + y_down_in[2].astype(f32)
    )
    grad_ref[:, :HALFT] = second[:OWN].astype(bf16)
    grad_ref[:, HALFT:] = second[OWN:].astype(bf16)
    h4[0].wait_recv()
    h4.append(send(hid_all.at[far_rows], hid_all.at[far_rows], to_core))
    for copy in a2:
        copy.wait_recv()
    for t in range(NT):
        both = adapters[t].astype(f32)
        tall[0, t * OWN : (t + 1) * OWN, :] = both[:OWN]
        tall[1, t * OWN : t * OWN + 40, :RANK] = both[OWN:, :RANK]
        tall[1, t * OWN + 40 : (t + 1) * OWN, :RANK] = both[OWN : OWN + 32, RANK:]
    turned = tall[0].T.astype(bf16)
    left_ref[0] = turned[:RANK]
    left_ref[1] = turned[RANK:]
    down_right_ref[...] = tall[1].T[:RANK].astype(bf16)
    h4[1].wait_recv()
    h4[2].wait_recv()
    turned = hid_all[...].astype(f32).T
    right_ref[0] = turned[:RANK].astype(bf16)
    right_ref[1] = turned[RANK : 2 * RANK].astype(bf16)
    down_left_ref[...] = turned[2 * RANK : 3 * RANK].astype(bf16)
    for copy in started:
        copy.wait_send()


def hand_over(*refs):
    for source, target in zip(refs[:6], refs[6:]):
        target[...] = source[...]


def on_device(
    tokens,
    cotangent,
    gate_up_weight,
    down_weight,
    gate_up_noise,
    down_noise,
    gate_up_left,
    gate_up_right,
    down_left,
    down_right,
):
    scale_grad = (NX * TOK) ** (-0.5)
    vmem, anywhere = pl.BlockSpec(memory_space=pltpu.VMEM), pl.BlockSpec(memory_space=pl.ANY)
    scratch = [
        pltpu.VMEM((3, HID, FEAT), bf16),
        pltpu.VMEM((3, HID, FEAT), bf16),
        pltpu.VMEM((3, FEAT, HID), bf16),
        pltpu.VMEM((2 * OWN, TOK), bf16),
        pltpu.VMEM((NT, 2 * OWN, HALFT), bf16),
        pltpu.VMEM((NT, 2 * OWN, HALFT), bf16),
        pltpu.VMEM((2, FEAT, TOK), bf16),
        pltpu.VMEM((3, FEAT, RANK), bf16),
        pltpu.VMEM((3, HID, RANK), bf16),
        pltpu.VMEM((3, RANK, HID), bf16),
        pltpu.VMEM((3, RANK, TOK), bf16),
        pltpu.VMEM((3 * RANK, TOK), bf16),
        pltpu.VMEM((2, 2, 3, HID, LANES), bf16),
        pltpu.VMEM((2, 3, HID, LANES), bf16),
        pltpu.VMEM((2, 3, HID, LANES), bf16),
        pltpu.VMEM((2, 3, HID, LANES), bf16),
        pltpu.VMEM((2, 2, 3, HID, LANES), bf16),
        pltpu.VMEM((FEAT, TOK), f32),
        pltpu.VMEM((FEAT, TOK), f32),
        pltpu.VMEM((NT, 2 * OWN, HALFT), bf16),
        pltpu.VMEM((4, 2, 2 * OWN, HALFT), bf16),
        pltpu.VMEM((4, 2, 2 * OWN, HALFT), bf16),
        pltpu.VMEM((2 * OWN, HALFT), bf16),
        pltpu.VMEM((NT, 2 * OWN, HALFT), bf16),
        pltpu.VMEM((NZ, 2 * OWN, HALFT), bf16),
        pltpu.VMEM((4, 2 * OWN, HALFT), bf16),
        pltpu.VMEM((3, 2 * OWN, HALFT), bf16),
        pltpu.VMEM((NT, 48, 128), bf16),
        pltpu.VMEM((NT, 48, 128), bf16),
        pltpu.VMEM((NT, 48, 128), bf16),
        pltpu.VMEM((NX, PACK, 2 * RANK), bf16),
        pltpu.VMEM((NT, PACK, 2 * RANK), bf16),
        pltpu.VMEM((2, FEAT, 2 * RANK), f32),
        pltpu.VMEM((HID, 4 * RANK), bf16),
        pltpu.VMEM((HID // 2, 4 * RANK), bf16),
        pltpu.VMEM((SHARD, 4 * RANK), bf16),
        pltpu.VMEM((SHARD, 4 * RANK), bf16),
        pltpu.VMEM((NX, SHARD, 4 * RANK), bf16),
        pltpu.VMEM((HID, 4 * RANK), bf16),
        pltpu.SemaphoreType.DMA((MESSAGES,)),
        pltpu.SemaphoreType.DMA((MESSAGES,)),
        pltpu.SemaphoreType.DMA((16,)),
    ]
    shapes = [
        (OWN, TOK),
        (OWN, TOK),
        (2, RANK, FEAT),
        (2, RANK, HID),
        (RANK, HID),
        (RANK, FEAT),
    ]
    shapes = tuple(jax.ShapeDtypeStruct(shape, bf16) for shape in shapes)
    results = pl.pallas_call(
        functools.partial(kernel, scale_grad),
        out_shape=shapes,
        in_specs=[vmem] * 2 + [anywhere] * 4 + [vmem] * 4,
        out_specs=(vmem,) * 6,
        scratch_shapes=scratch,
        compiler_params=pltpu.CompilerParams(
            collective_id=0, has_side_effects=True, vmem_limit_bytes=62 * 2**20
        ),
    )(
        tokens[0].T,
        cotangent[0].T,
        jnp.swapaxes(gate_up_weight, 1, 2),
        down_weight,
        gate_up_noise[0],
        down_noise[0],
        jnp.swapaxes(gate_up_left, 1, 2),
        gate_up_right,
        down_left.T,
        down_right,
    )
    out, grad, left, right, down_left_grad, down_right_grad = pl.pallas_call(
        hand_over, out_shape=shapes, in_specs=[vmem] * 6, out_specs=(vmem,) * 6
    )(*results)
    return (
        out.T[None],
        grad.T[None],
        jnp.swapaxes(left, 1, 2),
        right,
        down_left_grad.T,
        down_right_grad,
    )


def solution(mesh):
    in_specs = (
        P("draw", None, ("batch", "tensor")),
        P("draw", None, ("batch", "tensor")),
        P(None, "batch", ("tensor", "draw")),
        P(("tensor", "draw"), "batch"),
        P("draw", None, "batch", "tensor"),
        P("draw", "tensor", "batch"),
        P(None, "batch", None),
        P(None, None, "tensor"),
        P("tensor", None),
        P(None, "batch"),
    )
    out_specs = (
        P("draw", None, ("batch", "tensor")),
        P("draw", None, ("batch", "tensor")),
        P(None, "batch", None),
        P(None, None, "tensor"),
        P("tensor", None),
        P(None, "batch"),
    )
    return jax.shard_map(
        on_device, mesh=mesh, in_specs=in_specs, out_specs=out_specs, check_vma=False
    )
```

time: 151 us -> 137 us (0.907)
  Pallas kernels: 149 us -> 134 us
    pallas_call x1, Pallas kernels: 147 us -> 132 us  [on_device(): pl.pallas_call(functools.partial(kernel, scale_grad), out_shape=shapes, i...]
where the time goes in v4:
time: 137 us; the launch traced here: 135 us
  Pallas kernels  134 us (98%)
    pallas_call x1, Pallas kernels, on_device(): pl.pallas_call(functools.partial(kernel, scale_grad), out_shape=shapes, i...  132 us

profile of v4, /device:TPU:32, one launch (start us, length us, event | category | flops | bytes accessed | tf_op | source)
XLA Modules:
  0.0 134.5 jit_solution(6124330213257919434)
XLA Ops:
  0.6 131.7 %shard_map.145 = (bf16[72,512]{1,0:T(8,128)(2,1)}, bf16[72,512]{1,0:T(8,128)(2,1)}, bf16[2,64,1152]{2,1,0:T(8,128)(2,1)}, bf16[2,64,1152]{2,1,0:T(8,128)(2,1)}, ...) custom-call(bf16[72,512]{1,0:T(8,128)(2,1)} %bitcast.24, bf16[72,512]{1,0:T(8,128)(2,1)} %bitcast.25, ...), custom_call_target="tpu_custom_call" | custom-call | tf_op jit(solution)/shard_map/pallas_call | solution.py:764
  132.3 2.2 %shard_map.146 = (bf16[72,512]{1,0:T(8,128)(2,1)}, bf16[72,512]{1,0:T(8,128)(2,1)}, bf16[2,64,1152]{2,1,0:T(8,128)(2,1)}, bf16[2,64,1152]{2,1,0:T(8,128)(2,1)}, ...) custom-call(bf16[72,512]{1,0:T(8,128)(2,1)} %get-tuple-element.18.refs_0_, bf16[72,512]{1,0:T(8,128)(2,1)} %get-tuple-element.19.refs_1_, ...), custom_call_target="tpu_custom_call" | custom-call | tf_op jit(solution)/shard_map/pallas_call | solution.py:785

commit v5 on v4

--- a/solution.py
+++ b/solution.py
@@ -19,8 +19,6 @@
 SHARD = HID // NX
 HALF = SHARD // 2
 OWN = FEAT // NT
-PACK = OWN + 40
-LANES = TOK // 4
 PARTS = ((0, 80), (80, 64), (144, 80), (224, 64))
 PLACES = ((0, 80, 144, 224), (720, 800, 432, 512), (864, 1024, 944, 1088), (288, 368, 576, 656))
 BLOCKS = (
@@ -32,7 +30,9 @@
 )
 HALFT = TOK // 2
 EARLY = 768
-MESSAGES = 180
+LANES = TOK // 4
+MESSAGES = 216
+WIDE = 640
 
 
 def gelu_pair(value):
@@ -74,7 +74,6 @@
     weights,
     noisy,
     noisy_t,
-    own_acts,
     gathered,
     gathered_c,
     acts,
@@ -100,14 +99,16 @@
     y_down_in,
     rank_out,
     rank_in,
-    rank_all,
     draw_in,
     adapters,
-    tall,
-    hid_part,
-    hid_core,
-    hid_y_out,
-    hid_y_in,
+    down_rank_out,
+    down_rank_in,
+    down_draw_in,
+    down_adapters,
+    lows_core,
+    lows_y_out,
+    lows_y_in,
+    lows_all,
     hid_draw,
     hid_all,
     send_sem,
@@ -150,19 +151,17 @@
         started.append(copy)
         return copy
 
-    def side_by_side(value):
-        return jnp.concatenate([value[:, :HALFT], value[:, HALFT:]])
-
-    own_tokens, own_cotangent = tokens_in[...].astype(f32), cotangent_in[...].astype(f32)
-    own_acts[...] = jnp.concatenate([own_tokens, own_cotangent]).astype(bf16)
-    gathered[tensor] = side_by_side(own_tokens).astype(bf16)
-    gathered_c[tensor] = side_by_side(own_cotangent).astype(bf16)
-
     barrier = pltpu.get_barrier_semaphore()
     tensor_peers = [(tensor + o) % NT for o in range(1, NT)]
     partners = [*x_peers, to_core, y_hi, *({"tensor": peer} for peer in tensor_peers)]
     for where in partners:
         pl.semaphore_signal(barrier, inc=1, device_id=where, device_id_type=MESH)
+    def side_by_side(value):
+        return jnp.concatenate([value[:, :HALFT], value[:, HALFT:]])
+
+    own_tokens, own_cotangent = tokens_in[...].astype(f32), cotangent_in[...].astype(f32)
+    gathered[tensor] = side_by_side(own_tokens).astype(bf16)
+    gathered_c[tensor] = side_by_side(own_cotangent).astype(bf16)
     pl.semaphore_wait(barrier, len(partners))
 
     def rows(owner, first=0, size=SHARD):
@@ -365,22 +364,8 @@
     def all_tokens(k, first=0, last=HID):
         return jnp.concatenate([back[b % 2, b // 2, k, first:last, :] for b in range(4)], axis=1)
 
-    def hid_rows(j, ks, lanes):
-        start, size, parts = BLOCKS[j]
-        turned = [dot_nt(all_tokens(k, start, start + size), lows[k]) for k in ks]
-        turned = jnp.concatenate(turned, axis=1).astype(bf16)
-        at = 0
-        for shard, first, count in parts:
-            hid_part[rows(owners[shard], first, count), lanes] = turned[at : at + count]
-            at += count
-
-    def finish(j, copy):
-        copy.wait_recv()
-        hid_rows(j, (2, 2), slice(2 * RANK, 4 * RANK))
-
-    def finish_grad(j, copy):
-        copy.wait_recv()
-        hid_rows(j, (0, 1), slice(0, 2 * RANK))
+    def finish(copy):
+        copy.wait_recv()
 
     def early_outputs(m, _):
         at = pl.ds(pl.multiple_of(m * SHARD, 16), SHARD)
@@ -423,8 +408,75 @@
     next(rings)
     unpack(gathered_c, 1)
     lows[2] = dot(down_right_n[...], acts[1]).astype(bf16)
+    def select(shape, test):
+        row, column = (lax.broadcasted_iota(jnp.int32, shape, axis) for axis in (0, 1))
+        return jnp.where(test(row, column), 1.0, 0.0).astype(bf16)
+
+    def over_draws(ref):
+        total = (ref[0].astype(f32) + ref[1].astype(f32)) + (ref[2].astype(f32) + ref[3].astype(f32))
+        return (scale_grad * total).astype(bf16)
+
+    def sum_units(out, box):
+        total = out[tensor].astype(f32)
+        for o in range(NT - 1):
+            total = total + box[o].astype(f32)
+        return total
+
+    z_order = (1, 7, 2, 6, 3, 5, 4)
+
+    def spread_adapters(ref):
+        mine = ref.at[tensor]
+        near = [send(mine, mine, {"tensor": yl * NZ + ring(z + o, NZ)}) for o in z_order]
+        return near, [send(mine, mine, y_lo)]
+
+    def forward_adapters(ref, near, far, these):
+        for at in these:
+            near[at].wait_recv()
+            there = ref.at[yl * NZ + ring(z - z_order[at], NZ)]
+            far.append(send(there, there, y_lo))
+
+    def down_ranks():
+        chosen = select(
+            (16 * NT, RANK),
+            lambda row, column: jnp.logical_and(row % 16 < 4, column == row // 16 * 4 + row % 16),
+        )
+        boxed = dot(chosen, ranks[2 * RANK :, :]).astype(bf16)
+        for unit in range(NT):
+            down_rank_out[unit] = boxed[16 * unit : 16 * (unit + 1)]
+        return [
+            send(down_rank_out.at[peer], down_rank_in.at[o], {"tensor": peer})
+            for o, peer in enumerate(tensor_peers)
+        ]
+
+    def down_draws(copies):
+        for copy in copies:
+            copy.wait_recv()
+        total = sum_units(down_rank_out, down_rank_in).astype(bf16)
+        rows_f = dot_nt(total, acts[1]).astype(bf16)
+        third, folded = FEAT // 3, None
+        for q in range(3):
+            chosen = select(
+                (16, 16),
+                lambda row, column: jnp.logical_and(row == column + 4 * q, column < 4),
+            )
+            piece = dot(chosen, rows_f[:, q * third : (q + 1) * third])
+            folded = piece if folded is None else folded + piece
+        down_draw_in[x] = folded.astype(bf16)
+        mine = down_draw_in.at[x]
+        return [send(mine, mine, where) for where in x_peers]
+
+    def down_spread(copies):
+        for copy in copies:
+            copy.wait_recv()
+        down_adapters[tensor] = over_draws(down_draw_in)
+        return spread_adapters(down_adapters)
+
+    low_sum = send(lows, lows_core, to_core)
     d0 = spread(0, 2, 3)
     g0 = bend(0, g0)
+    low_sum.wait_recv()
+    lows_y_out[...] = (lows[...].astype(f32) + lows_core[...].astype(f32)).astype(bf16)
+    low_sum = send(lows_y_out, lows_y_in, y_hi)
     d0 = cores(0, 2, 3, d0)
     for copy in last[:4]:
         copy.wait_recv()
@@ -432,11 +484,13 @@
     flip_back(0, 2, 0, 6)
     g3 = cores(3, 0, 2, g3)
     g1 = bend(1, g1)
-    finish(0, g0)
+    finish(g0)
+    low_sum.wait_recv()
+    lows_all[...] = (lows_y_out[...].astype(f32) + lows_y_in[...].astype(f32)).astype(bf16)
     for copy in last[4:8]:
         copy.wait_recv()
     g4 = spread(4, 0, 2)
-    finish(1, g1)
+    finish(g1)
     g4 = cores(4, 0, 2, g4)
     flip_back(0, 2, 6, 9)
     g2 = bend(2, g2)
@@ -446,11 +500,11 @@
     forward(2, 80, 64)
     d1 = spread(1, 2, 3)
     d0 = bend_grad(0, d0)
-    finish(2, g2)
+    finish(g2)
     d1 = cores(1, 2, 3, d1)
     g3 = bend(3, g3)
-    finish_grad(0, d0)
-    finish(3, g3)
+    finish(d0)
+    finish(g3)
     to_right[5].wait_recv()
     to_left[5].wait_recv()
     d2 = spread(2, 2, 3)
@@ -458,12 +512,13 @@
     d2 = cores(2, 2, 3, d2)
     flip_back(2, 3, 0, 6)
     lax.fori_loop(0, 4, early_outputs, 0)
-    finish(4, g4)
+    finish(g4)
     for copy in last[8:10]:
         copy.wait_recv()
     d3 = spread(3, 2, 3)
     d1 = bend_grad(1, d1)
     ranks[pl.ds(2 * RANK, RANK), :] = dot(right_a[2], all_tokens(2)).astype(bf16)
+    down_sums = down_ranks()
     d3 = cores(3, 2, 3, d3)
     for copy in last[10:]:
         copy.wait_recv()
@@ -501,30 +556,49 @@
     go(1, 1, True)
     go(1, 0, False)
     d2 = bend_grad(2, d2)
-    finish_grad(1, d1)
-    finish_grad(2, d2)
+    down_sums = down_draws(down_sums)
+    finish(d1)
+    finish(d2)
     d3 = bend_grad(3, d3)
     go(1, 0, True)
     go(1, 1, False)
     lax.fori_loop(0, 4, early_grads, 0)
     d4 = bend_grad(4, d4)
-    finish_grad(3, d3)
-    finish_grad(4, d4)
-
-    full = jnp.concatenate([dot(right_a[k], all_tokens(k)) for k in (0, 1)]).astype(bf16)
-    ranks[: 2 * RANK, :] = full
-    full = jnp.concatenate([full, ranks[2 * RANK :, :]])
+    down_near, down_far = down_spread(down_sums)
+    finish(d3)
+    finish(d4)
+
+    for k in (0, 1):
+        ranks[pl.ds(k * RANK, RANK), :] = dot(right_a[k], all_tokens(k)).astype(bf16)
+    halves = []
+    for half in (0, 1):
+        chosen = select(
+            (8 * NT, 2 * RANK),
+            lambda row, column: column == row % 8 // 4 * RANK + row // 8 * 4 + row % 4,
+        )
+        halves.append(dot(chosen, ranks[: 2 * RANK, half * HALFT : (half + 1) * HALFT]))
     for unit in range(NT):
-        down, across = unit // 4 * 48, unit % 4 * 128
-        rank_out[unit] = full[down : down + 48, across : across + 128]
+        at = slice(8 * unit, 8 * (unit + 1))
+        rank_out[unit] = jnp.concatenate([halves[0][at], halves[1][at]]).astype(bf16)
     r1 = [
         send(rank_out.at[peer], rank_in.at[o], {"tensor": peer})
         for o, peer in enumerate(tensor_peers)
     ]
 
-    h1 = send(
-        hid_part.at[pl.ds(pl.multiple_of((1 - core) * 576, 16), 576)], hid_core, to_core
-    )
+    quarter = core * 2 + yh
+    for piece, (first, size) in enumerate(PARTS):
+        at = place(quarter, piece)
+        turned = [
+            dot_nt(
+                jnp.concatenate([back[b % 2, b // 2, k, at, :] for b in range(4)], axis=1),
+                lows_all[k],
+            )
+            for k in (0, 1, 2, 2)
+        ]
+        hid_draw[x, pl.ds(first, size), :] = jnp.concatenate(turned, axis=1).astype(bf16)
+    h3 = [send(hid_draw.at[x], hid_draw.at[x], where) for where in x_peers]
+    own_rows = pl.ds(pl.multiple_of(quarter * SHARD, 16), SHARD)
+    far_rows = pl.ds(pl.multiple_of((core * 2 + 1 - yh) * SHARD, 16), SHARD)
 
     def grads(half, group):
         m = half * 2 + group
@@ -562,43 +636,34 @@
     go(2, 1, False)
     for copy in r1:
         copy.wait_recv()
-    total = rank_out[tensor].astype(f32)
-    for o in range(NT - 1):
-        total = total + rank_in[o].astype(f32)
-    rank_all[tensor] = total.astype(bf16)
-    r2 = [
-        send(rank_all.at[tensor], rank_all.at[tensor], {"tensor": peer}) for peer in tensor_peers
-    ]
+    total = sum_units(rank_out, rank_in)
+    total = jnp.concatenate([total[:8], total[8:]], axis=1).astype(bf16)
+    total = jnp.concatenate([total.astype(f32)] * 2).astype(bf16)
+    rows_f = dot_nt(total, acts[0])
+    rest = jnp.concatenate([rows_f[8:, WIDE:], rows_f[8:, : 2 * WIDE - FEAT]], axis=1)
+    draw_in[x] = jnp.concatenate([rows_f[:8, :WIDE], rest]).astype(bf16)
+    d1 = [send(draw_in.at[x], draw_in.at[x], where) for where in x_peers]
     y_up = y_pass(0, True, None, crossed[4])
     go(3, 1, True)
     go(3, 0, False)
-
-    h1.wait_recv()
-    own_rows = pl.ds(pl.multiple_of(core * 576 + yh * SHARD, 16), SHARD)
-    far_rows = pl.ds(pl.multiple_of(core * 576 + (1 - yh) * SHARD, 16), SHARD)
-    own_half = pl.ds(pl.multiple_of(yh * SHARD, 16), SHARD)
-    far_half = pl.ds(pl.multiple_of((1 - yh) * SHARD, 16), SHARD)
-    hid_y_out[...] = (
-        hid_part[far_rows, :].astype(f32) + hid_core[far_half, :].astype(f32)
-    ).astype(bf16)
-    h2 = send(hid_y_out, hid_y_in, y_hi)
-
     y_down = y_pass(0, False, None, crossed[-3])
     go(3, 0, True)
     go(3, 1, False)
+    for copy in d1:
+        copy.wait_recv()
+    adapters[tensor] = over_draws(draw_in)
+    near, far = spread_adapters(adapters)
+    forward_adapters(down_adapters, down_near, down_far, range(7))
     y_up = y_pass(1, True, y_up, crossed[3])
-
-    for copy in r2:
-        copy.wait_recv()
-    full = jnp.concatenate(
-        [jnp.concatenate([rank_all[4 * r + c] for c in range(4)], axis=1) for r in range(4)]
-    )
-    both = dot_nt(own_acts[...], full)
-    third = both[OWN:, 2 * RANK :]
-    folded = jnp.concatenate([third[40:], jnp.zeros((8, RANK), f32)])
-    folded = jnp.concatenate([third[:40], folded], axis=1)
-    draw_in[x] = jnp.concatenate([both[:OWN, : 2 * RANK], folded]).astype(bf16)
-    d1 = [send(draw_in.at[x], draw_in.at[x], where) for where in x_peers]
+    y_down = y_pass(1, False, y_down, crossed[-2])
+
+    for copy in h3:
+        copy.wait_recv()
+    hid_all[own_rows, :] = over_draws(hid_draw)
+    h4 = [
+        send(hid_all.at[own_rows], hid_all.at[own_rows], y_hi),
+        send(hid_all.at[own_rows], hid_all.at[own_rows], to_core),
+    ]
 
     for copy in flight.values():
         copy.wait_recv()
@@ -613,49 +678,18 @@
     y_piece = (1 - yl) * NZ + z
     pieces[y_piece] = over_z(1 - yl).astype(bf16)
     cross = send(pieces.at[y_piece], cross_in, y_lo)
-    y_down = y_pass(1, False, y_down, crossed[-2])
     y_up = y_pass(2, True, y_up, crossed[2])
-
-    def over_draws(ref):
-        total = (ref[0].astype(f32) + ref[1].astype(f32)) + (ref[2].astype(f32) + ref[3].astype(f32))
-        return (scale_grad * total).astype(bf16)
-
-    for copy in d1:
-        copy.wait_recv()
-    adapters[tensor] = over_draws(draw_in)
-    mine = adapters.at[tensor]
-    a1 = [
-        send(mine, mine, {"tensor": yl * NZ + ring(z + o, NZ)}) for o in (1, 7, 2, 6, 3, 5, 4)
-    ]
-    a2 = [send(mine, mine, y_lo)]
-
     y_down = y_pass(2, False, y_down, crossed[-1])
     y_up = y_pass(3, True, y_up, crossed[1])
 
-    h2.wait_recv()
-    hid_draw[x] = (
-        hid_part[own_rows, :].astype(f32)
-        + hid_core[own_half, :].astype(f32)
-        + hid_y_in[...].astype(f32)
-    ).astype(bf16)
-    h3 = [send(hid_draw.at[x], hid_draw.at[x], where) for where in x_peers]
-
+    forward_adapters(adapters, near, far, range(4))
+    h4[0].wait_recv()
+    h4.append(send(hid_all.at[far_rows], hid_all.at[far_rows], to_core))
     cross.wait_recv()
     first = over_z(yl) + cross_in[...].astype(f32)
     out_ref[:, :HALFT] = first[:OWN].astype(bf16)
     out_ref[:, HALFT:] = first[OWN:].astype(bf16)
-    for o, copy in zip((1, 7, 2, 6, 3, 5, 4), a1):
-        copy.wait_recv()
-        at = adapters.at[yl * NZ + ring(z - o, NZ)]
-        a2.append(send(at, at, y_lo))
-
-    for copy in h3:
-        copy.wait_recv()
-    hid_all[own_rows, :] = over_draws(hid_draw)
-    h4 = [
-        send(hid_all.at[own_rows], hid_all.at[own_rows], y_hi),
-        send(hid_all.at[own_rows], hid_all.at[own_rows], to_core),
-    ]
+    forward_adapters(adapters, near, far, range(4, 7))
     y_up.wait_recv()
     y_down.wait_recv()
     crossed[0].wait_recv()
@@ -666,25 +700,35 @@
     )
     grad_ref[:, :HALFT] = second[:OWN].astype(bf16)
     grad_ref[:, HALFT:] = second[OWN:].astype(bf16)
-    h4[0].wait_recv()
-    h4.append(send(hid_all.at[far_rows], hid_all.at[far_rows], to_core))
-    for copy in a2:
-        copy.wait_recv()
-    for t in range(NT):
-        both = adapters[t].astype(f32)
-        tall[0, t * OWN : (t + 1) * OWN, :] = both[:OWN]
-        tall[1, t * OWN : t * OWN + 40, :RANK] = both[OWN:, :RANK]
-        tall[1, t * OWN + 40 : (t + 1) * OWN, :RANK] = both[OWN : OWN + 32, RANK:]
-    turned = tall[0].T.astype(bf16)
-    left_ref[0] = turned[:RANK]
-    left_ref[1] = turned[RANK:]
-    down_right_ref[...] = tall[1].T[:RANK].astype(bf16)
     h4[1].wait_recv()
     h4[2].wait_recv()
     turned = hid_all[...].astype(f32).T
     right_ref[0] = turned[:RANK].astype(bf16)
     right_ref[1] = turned[RANK : 2 * RANK].astype(bf16)
     down_left_ref[...] = turned[2 * RANK : 3 * RANK].astype(bf16)
+    for copy in down_far:
+        copy.wait_recv()
+    stacked = jnp.concatenate([down_adapters[unit] for unit in range(NT)])
+    for q in range(3):
+        chosen = select(
+            (RANK, 16 * NT), lambda row, column: column == row // 4 * 16 + row % 4 + 4 * q
+        )
+        third = slice(q * FEAT // 3, (q + 1) * FEAT // 3)
+        down_right_ref[:, third] = dot(chosen, stacked).astype(bf16)
+    for copy in far:
+        copy.wait_recv()
+    stacked = jnp.concatenate([adapters[unit] for unit in range(NT)])
+    for q in (0, 1):
+        chosen = select(
+            (2 * RANK, 16 * NT),
+            lambda row, column: column
+            == row % RANK // 4 * 16 + row // RANK * 4 + row % 4 + 8 * q,
+        )
+        wide = WIDE if q == 0 else FEAT - WIDE
+        turned = dot(chosen, stacked[:, :wide]).astype(bf16)
+        at = slice(q * WIDE, q * WIDE + wide)
+        left_ref[0, :, at] = turned[:RANK]
+        left_ref[1, :, at] = turned[RANK:]
     for copy in started:
         copy.wait_send()
 
@@ -712,7 +756,6 @@
         pltpu.VMEM((3, HID, FEAT), bf16),
         pltpu.VMEM((3, HID, FEAT), bf16),
         pltpu.VMEM((3, FEAT, HID), bf16),
-        pltpu.VMEM((2 * OWN, TOK), bf16),
         pltpu.VMEM((NT, 2 * OWN, HALFT), bf16),
         pltpu.VMEM((NT, 2 * OWN, HALFT), bf16),
         pltpu.VMEM((2, FEAT, TOK), bf16),
@@ -736,16 +779,18 @@
         pltpu.VMEM((NZ, 2 * OWN, HALFT), bf16),
         pltpu.VMEM((4, 2 * OWN, HALFT), bf16),
         pltpu.VMEM((3, 2 * OWN, HALFT), bf16),
-        pltpu.VMEM((NT, 48, 128), bf16),
-        pltpu.VMEM((NT, 48, 128), bf16),
-        pltpu.VMEM((NT, 48, 128), bf16),
-        pltpu.VMEM((NX, PACK, 2 * RANK), bf16),
-        pltpu.VMEM((NT, PACK, 2 * RANK), bf16),
-        pltpu.VMEM((2, FEAT, 2 * RANK), f32),
-        pltpu.VMEM((HID, 4 * RANK), bf16),
-        pltpu.VMEM((HID // 2, 4 * RANK), bf16),
-        pltpu.VMEM((SHARD, 4 * RANK), bf16),
-        pltpu.VMEM((SHARD, 4 * RANK), bf16),
+        pltpu.VMEM((NT, 16, HALFT), bf16),
+        pltpu.VMEM((NT, 16, HALFT), bf16),
+        pltpu.VMEM((NX, 16, WIDE), bf16),
+        pltpu.VMEM((NT, 16, WIDE), bf16),
+        pltpu.VMEM((NT, 16, TOK), bf16),
+        pltpu.VMEM((NT, 16, TOK), bf16),
+        pltpu.VMEM((NX, 16, FEAT // 3), bf16),
+        pltpu.VMEM((NT, 16, FEAT // 3), bf16),
+        pltpu.VMEM((3, RANK, TOK), bf16),
+        pltpu.VMEM((3, RANK, TOK), bf16),
+        pltpu.VMEM((3, RANK, TOK), bf16),
+        pltpu.VMEM((3, RANK, TOK), bf16),
         pltpu.VMEM((NX, SHARD, 4 * RANK), bf16),
         pltpu.VMEM((HID, 4 * RANK), bf16),
         pltpu.SemaphoreType.DMA((MESSAGES,)),

time: 137 us -> 128 us (0.934)
  Pallas kernels: 134 us -> 126 us
    pallas_call x1, Pallas kernels: 132 us -> 124 us  [on_device(): pl.pallas_call(functools.partial(kernel, scale_grad), out_shape=shapes, i...]
where the time goes in v5:
time: 128 us; the launch traced here: 127 us
  Pallas kernels  126 us (98%)
    pallas_call x1, Pallas kernels, on_device(): pl.pallas_call(functools.partial(kernel, scale_grad), out_shape=shapes, i...  124 us

profile of v5, /device:TPU:32, one launch (start us, length us, event | category | flops | bytes accessed | tf_op | source)
XLA Modules:
  0.0 126.6 jit_solution(13241263419988166601)
XLA Ops:
  0.6 123.7 %shard_map.145 = (bf16[72,512]{1,0:T(8,128)(2,1)}, bf16[72,512]{1,0:T(8,128)(2,1)}, bf16[2,64,1152]{2,1,0:T(8,128)(2,1)}, bf16[2,64,1152]{2,1,0:T(8,128)(2,1)}, ...) custom-call(bf16[72,512]{1,0:T(8,128)(2,1)} %bitcast.24, bf16[72,512]{1,0:T(8,128)(2,1)} %bitcast.25, ...), custom_call_target="tpu_custom_call" | custom-call | tf_op jit(solution)/shard_map/pallas_call | solution.py:809
  124.4 2.2 %shard_map.146 = (bf16[72,512]{1,0:T(8,128)(2,1)}, bf16[72,512]{1,0:T(8,128)(2,1)}, bf16[2,64,1152]{2,1,0:T(8,128)(2,1)}, bf16[2,64,1152]{2,1,0:T(8,128)(2,1)}, ...) custom-call(bf16[72,512]{1,0:T(8,128)(2,1)} %get-tuple-element.18.refs_0_, bf16[72,512]{1,0:T(8,128)(2,1)} %get-tuple-element.19.refs_1_, ...), custom_call_target="tpu_custom_call" | custom-call | tf_op jit(solution)/shard_map/pallas_call | solution.py:830

commit v6 on v5

--- a/solution.py
+++ b/solution.py
@@ -438,7 +438,7 @@
     def down_ranks():
         chosen = select(
             (16 * NT, RANK),
-            lambda row, column: jnp.logical_and(row % 16 < 4, column == row // 16 * 4 + row % 16),
+            lambda row, column: jnp.logical_and((row & 15) < 4, column == (row >> 4) * 4 + (row & 15)),
         )
         boxed = dot(chosen, ranks[2 * RANK :, :]).astype(bf16)
         for unit in range(NT):
@@ -517,14 +517,14 @@
         copy.wait_recv()
     d3 = spread(3, 2, 3)
     d1 = bend_grad(1, d1)
-    ranks[pl.ds(2 * RANK, RANK), :] = dot(right_a[2], all_tokens(2)).astype(bf16)
-    down_sums = down_ranks()
     d3 = cores(3, 2, 3, d3)
     for copy in last[10:]:
         copy.wait_recv()
     d4 = spread(4, 2, 3)
+    ranks[pl.ds(2 * RANK, RANK), :] = dot(right_a[2], all_tokens(2)).astype(bf16)
     flip_back(2, 3, 6, 9)
     d4 = cores(4, 2, 3, d4)
+    down_sums = down_ranks()
 
     def outputs(half, group):
         m = half * 2 + group
@@ -556,15 +556,13 @@
     go(1, 1, True)
     go(1, 0, False)
     d2 = bend_grad(2, d2)
-    down_sums = down_draws(down_sums)
     finish(d1)
     finish(d2)
     d3 = bend_grad(3, d3)
+    lax.fori_loop(0, 4, early_grads, 0)
+    d4 = bend_grad(4, d4)
     go(1, 0, True)
     go(1, 1, False)
-    lax.fori_loop(0, 4, early_grads, 0)
-    d4 = bend_grad(4, d4)
-    down_near, down_far = down_spread(down_sums)
     finish(d3)
     finish(d4)
 
@@ -574,7 +572,7 @@
     for half in (0, 1):
         chosen = select(
             (8 * NT, 2 * RANK),
-            lambda row, column: column == row % 8 // 4 * RANK + row // 8 * 4 + row % 4,
+            lambda row, column: column == ((row & 7) >> 2) * RANK + (row >> 3) * 4 + (row & 3),
         )
         halves.append(dot(chosen, ranks[: 2 * RANK, half * HALFT : (half + 1) * HALFT]))
     for unit in range(NT):
@@ -629,6 +627,7 @@
     crossed = {4: cross_y(z + 4)}
     go(2, 1, True)
     go(2, 0, False)
+    down_sums = down_draws(down_sums)
     lax.fori_loop(0, 2, grads, z // 4)
     for away in (3, -3, 2, -2, 1, -1, 0):
         crossed[away] = cross_y(z + away)
@@ -643,6 +642,7 @@
     rest = jnp.concatenate([rows_f[8:, WIDE:], rows_f[8:, : 2 * WIDE - FEAT]], axis=1)
     draw_in[x] = jnp.concatenate([rows_f[:8, :WIDE], rest]).astype(bf16)
     d1 = [send(draw_in.at[x], draw_in.at[x], where) for where in x_peers]
+    down_near, down_far = down_spread(down_sums)
     y_up = y_pass(0, True, None, crossed[4])
     go(3, 1, True)
     go(3, 0, False)
@@ -711,7 +711,7 @@
     stacked = jnp.concatenate([down_adapters[unit] for unit in range(NT)])
     for q in range(3):
         chosen = select(
-            (RANK, 16 * NT), lambda row, column: column == row // 4 * 16 + row % 4 + 4 * q
+            (RANK, 16 * NT), lambda row, column: column == (row >> 2) * 16 + (row & 3) + 4 * q
         )
         third = slice(q * FEAT // 3, (q + 1) * FEAT // 3)
         down_right_ref[:, third] = dot(chosen, stacked).astype(bf16)
@@ -722,7 +722,7 @@
         chosen = select(
             (2 * RANK, 16 * NT),
             lambda row, column: column
-            == row % RANK // 4 * 16 + row // RANK * 4 + row % 4 + 8 * q,
+            == ((row & 63) >> 2) * 16 + (row >> 6) * 4 + (row & 3) + 8 * q,
         )
         wide = WIDE if q == 0 else FEAT - WIDE
         turned = dot(chosen, stacked[:, :wide]).astype(bf16)

time: 128 us -> 127 us (level)
  no operation moved by 1% of the time
where the time goes in v6:
time: 127 us; the launch traced here: 126 us
  Pallas kernels  125 us (98%)
    pallas_call x1, Pallas kernels, on_device(): pl.pallas_call(functools.partial(kernel, scale_grad), out_shape=shapes, i...  123 us

profile of v6, /device:TPU:32, one launch (start us, length us, event | category | flops | bytes accessed | tf_op | source)
XLA Modules:
  0.0 125.9 jit_solution(10023238763751071228)
XLA Ops:
  0.6 123.1 %shard_map.145 = (bf16[72,512]{1,0:T(8,128)(2,1)}, bf16[72,512]{1,0:T(8,128)(2,1)}, bf16[2,64,1152]{2,1,0:T(8,128)(2,1)}, bf16[2,64,1152]{2,1,0:T(8,128)(2,1)}, ...) custom-call(bf16[72,512]{1,0:T(8,128)(2,1)} %bitcast.24, bf16[72,512]{1,0:T(8,128)(2,1)} %bitcast.25, ...), custom_call_target="tpu_custom_call" | custom-call | tf_op jit(solution)/shard_map/pallas_call | solution.py:809
  123.8 2.2 %shard_map.146 = (bf16[72,512]{1,0:T(8,128)(2,1)}, bf16[72,512]{1,0:T(8,128)(2,1)}, bf16[2,64,1152]{2,1,0:T(8,128)(2,1)}, bf16[2,64,1152]{2,1,0:T(8,128)(2,1)}, ...) custom-call(bf16[72,512]{1,0:T(8,128)(2,1)} %get-tuple-element.18.refs_0_, bf16[72,512]{1,0:T(8,128)(2,1)} %get-tuple-element.19.refs_1_, ...), custom_call_target="tpu_custom_call" | custom-call | tf_op jit(solution)/shard_map/pallas_call | solution.py:830
